TPU v7x, 32 devices: a whole 2x2x4 slice. The times are simulated.
32 devices in a mesh: site: 2 (over y), pt: 4 (over z), var: 2 (over x), cmp: 2 (over core).
Axes of the slice: x: 2, y: 2, z: 4, core: 2. Of those that a mesh axis runs over, the one named last changes fastest.
Arguments:
- strain_green: bfloat16 [5120, 24, 256], P(('site', 'pt'), None, 'cmp'), parts along dimension 0, may hold values from -2.390625 to 2.390625
- green_scale: float32 [40, 24], P(('site', 'pt')), parts along dimension 0, may hold values from 0.3 to 3
- mechanism: float32 [6, 2560], P(None, 'pt'), may hold values from -4 to 4
- slip_amplitude: bfloat16 [4, 32, 1536], P('pt', 'var'), may hold values from 0.19921875 to 2
- onset_time: float32 [4, 32, 1536], P('pt', 'var'), may hold values from 0 to 128
- rupture_row: int32 [4], replicated, may hold values from 0 to 3, each once
- rupture_blocks: int32 [4, 12], replicated, may hold values from 0 to 19, as said below
- block_count: int32 [4], replicated, may hold values from 1 to 12, 16 in all
- crossover: int32 [4], replicated, may hold values from 128 to 251
- high_band: float32 [8, 32, 2, 512], P(('site', 'pt'), 'var', None, 'cmp'), parts along dimension 0, may hold values from -6 to 6
Outputs:
- seismograms: float32 [8, 32, 2, 512], P(('site', 'pt'), 'var', None, 'cmp'), parts along dimension 0
There are 2 independent parts, one for each index of `site`. A program takes and returns all parts, laid end to end along the dimension named above; an argument that names none is the same for every part. Nothing has to cross between parts.
Inputs may be any that keep to these rules, and one draw needn't show every extreme that they name: `rupture_blocks`: each row names 12 different point blocks; rupture r covers the first block_count[r] of them.
All inputs are finite; a program needn't handle non-finite values.
Results may differ from a plain program's by a relative error of at most 0.0028.
Values may be sent and summed in bfloat16 or wider, within the bound.
No kernel may reach another device: no remote copies, remote signals or barrier semaphores. Data moves between devices by JAX's collectives and lax.ppermute only.
A program may use at most 64 MiB of HBM per device.

v0:
```python
import functools
import math

import jax
import jax.numpy as jnp
import ml_dtypes
import numpy as np
from jax import lax
from jax.experimental import pallas as pl
from jax.experimental.pallas import tpu as pltpu
from jax.sharding import PartitionSpec as P

taper_width = 8.0
f32 = jnp.float32
bf16 = jnp.bfloat16
highest = lax.Precision.HIGHEST
vmem_bytes = 32 * 1024 * 1024
SMEM = pl.BlockSpec(memory_space=pltpu.SMEM)
VMEM = pl.BlockSpec(memory_space=pltpu.VMEM)
HBM = pl.BlockSpec(memory_space=pltpu.HBM)


def in_hbm(*arrays):
    return [pltpu.with_memory_space_constraint(array, pltpu.HBM) for array in arrays]


def fetch(sources, targets, sems):
    copies = [
        pltpu.make_async_copy(source, target, sems.at[i])
        for i, (source, target) in enumerate(zip(sources, targets))
    ]
    for copy in copies:
        copy.start()
    return copies


def params():
    return pltpu.CompilerParams(vmem_limit_bytes=vmem_bytes)


def cost(flops, nbytes):
    return pl.CostEstimate(flops=flops, bytes_accessed=nbytes, transcendentals=0)


def split_table(table):
    high = table.astype(ml_dtypes.bfloat16)
    low = (table - high.astype(np.float64)).astype(ml_dtypes.bfloat16)
    return high, low


def fourier_table(bins, samples, samples_here):
    product = (np.arange(bins)[:, None] * np.arange(samples_here)[None, :]) % samples
    angle = product * (2.0 * np.pi / samples)
    return np.concatenate([np.cos(angle), -np.sin(angle)], axis=0)


def scalar_scratch(arrays):
    return [pltpu.SMEM(array.shape, array.dtype) for array in arrays]


def live_words(pt_size, blocks_here):
    steps_per_word = 30 // blocks_here
    return steps_per_word, pl.cdiv(pt_size, steps_per_word)


def pack_kernel(blocks_here, block_points, onset_scale, slip_scale, *refs):
    sources, strain_hbm, outs = refs[:5], refs[5], refs[6:-9]
    live_ref, head_ref, targets, sems, head_sem = refs[-9], refs[-8], refs[-7:-2], refs[-2], refs[-1]
    row_ref, blocks_ref, count_ref, slip_ref, onset_ref = targets
    copies = fetch(sources, targets, sems)
    head = pltpu.make_async_copy(strain_hbm.at[pl.ds(0, head_ref.shape[0])], head_ref, head_sem)
    head.start()
    for copy in copies[:3]:
        copy.wait()
    me = lax.axis_index("pt")
    rupture = row_ref[me]
    steps_per_word, words = live_words(len(outs), blocks_here)
    for word in range(words):

        def one_step(step, flags):
            other = row_ref[jnp.bitwise_xor(me, step)]

            def one_slot(slot, flags):
                local = blocks_ref[other, slot] - me * blocks_here
                bit = jnp.left_shift(1, local + (step - word * steps_per_word) * blocks_here)
                return jnp.where((local >= 0) & (local < blocks_here), flags | bit, flags)

            return lax.fori_loop(0, count_ref[other], one_slot, flags)

        last = min(len(outs), (word + 1) * steps_per_word)
        flags = lax.fori_loop(word * steps_per_word, last, one_step, 0)
        live_ref[word] = jnp.full(live_ref.shape[1:], flags, jnp.int32)
    for copy in copies[3:]:
        copy.wait()

    def visit(slot, carry):
        block = blocks_ref[rupture, slot]
        owner = block // blocks_here
        local = block - owner * blocks_here
        offset = pl.multiple_of(slot * block_points, block_points)
        onset = jnp.round(onset_ref[0, :, pl.ds(offset, block_points)] * onset_scale)
        onset = jnp.clip(onset.astype(jnp.int32) - 32768, -32768, 32767).astype(jnp.int16)
        slip = slip_ref[0, :, pl.ds(offset, block_points)].astype(f32) * slip_scale
        slip = slip.astype(jnp.int32).astype(jnp.int16)
        for step, out in enumerate(outs):

            @pl.when(owner == jnp.bitwise_xor(me, step))
            def _():
                out[local, 0] = onset
                out[local, 1] = slip

        return carry

    lax.fori_loop(0, count_ref[rupture], visit, 0)
    head.wait()


def three_parts(values):
    parts = []
    for _ in range(3):
        parts.append(values.astype(bf16).astype(f32))
        values = values - parts[-1]
    return parts


def green_kernel(
    steps, live_ref, head_ref, strain_hbm, scale_hbm, mechanism_hbm, out_ref, strain_ref, factor_ref, scale_ref, mechanism_ref, sems, small_sems
):
    small = fetch((scale_hbm, mechanism_hbm), (scale_ref, mechanism_ref), small_sems)
    rows, octet = 24, 8
    wide, depth = octet * rows, factor_ref.shape[1]
    blocks_here = scale_ref.shape[0]
    bins = strain_ref.shape[2]
    block_points = mechanism_ref.shape[1] // blocks_here
    per_block = block_points * rows

    def strain_copy(b, source=strain_hbm):
        place = pl.ds(pl.multiple_of(b * per_block, per_block), per_block)
        target = strain_ref.at[b, pl.ds(0, per_block)]
        return pltpu.make_async_copy(source.at[place], target, sems.at[b])

    for b in range(blocks_here):
        strain_copy(b, head_ref if b * per_block < head_ref.shape[0] else strain_hbm).start()
    for b in range(blocks_here):
        strain_ref[b, per_block:, :] = jnp.zeros((depth - wide, bins), bf16)
    for copy in small:
        copy.wait()
    column = lax.broadcasted_iota(jnp.int32, (18, depth), 1) % rows
    spread_six = column % 6 == lax.broadcasted_iota(jnp.int32, (18, depth), 0) % 6
    column = lax.broadcasted_iota(jnp.int32, (3 * rows, depth), 1) % rows
    spread_rows = column == lax.broadcasted_iota(jnp.int32, (3 * rows, depth), 0) % rows
    moments = lax.dot_general(
        jnp.concatenate(three_parts(mechanism_ref[...]), axis=0).astype(bf16),
        spread_six.astype(f32).astype(bf16),
        (((0,), (0,)), ((), ())),
        preferred_element_type=f32,
    )
    scales = jnp.dot(
        jnp.concatenate(three_parts(scale_ref[...]), axis=1).astype(bf16),
        spread_rows.astype(f32).astype(bf16),
        preferred_element_type=f32,
    )
    for b in range(blocks_here):
        place = slice(b * block_points, (b + 1) * block_points)
        factor_ref[place, :] = moments[place] * scales[b : b + 1]
    row = lax.broadcasted_iota(jnp.int32, (2 * octet, depth), 0)
    column = lax.broadcasted_iota(jnp.int32, (2 * octet, depth), 1)
    same_point = column // rows == row % octet
    part = (column % rows) // 6
    masks = [
        jnp.where(same_point & (part == 2 * h + row // octet), 1.0, 0.0).astype(bf16)
        for h in range(2)
    ]
    lane = lax.broadcasted_iota(jnp.int32, (2 * octet, bins), 1) % 4
    even, low_lane = lane % 2 == 0, lane < 2

    def shift(values, by):
        return pltpu.roll(values, by % bins, 1)

    steps_per_word, words = live_words(steps, blocks_here)
    live = [jnp.max(live_ref[word]) for word in range(words)]

    def one_block(b, carry):
        strain_copy(b).wait()
        flags = 0
        for step in range(steps):
            place = step % steps_per_word * blocks_here + b
            flags = flags | jnp.right_shift(live[step // steps_per_word], place)

        @pl.when(flags & 1 == 1)
        def _():
            place_block(b)

        return carry

    def place_block(b):
        for pair in range(block_points // (2 * octet)):
            spectra = [[], [], [], []]
            for half in range(2):
                first = pl.multiple_of(
                    b * block_points + pair * 2 * octet + half * octet, octet
                )
                here = factor_ref[pl.ds(first, octet)]
                here = jnp.concatenate([here, here], axis=0)
                coarse = here.astype(bf16)
                fine = (here - coarse.astype(f32)).astype(bf16)
                left = jnp.concatenate(
                    [coarse * masks[0], coarse * masks[1], fine * masks[0], fine * masks[1]],
                    axis=0,
                )
                own = (pair * 2 + half) * wide
                strain = strain_ref[b, own : own + depth, :]
                both = jnp.dot(left, strain, preferred_element_type=f32)
                for k in range(4):
                    spectra[k].append(
                        both[k * octet : (k + 1) * octet]
                        + both[(k + 4) * octet : (k + 5) * octet]
                    )
            green = [jnp.concatenate(s, axis=0).astype(bf16).astype(f32) for s in spectra]
            place = pl.ds(pair * 2 * octet, 2 * octet)
            below = pl.ds(block_points + pair * 2 * octet, 2 * octet)
            crossed = []
            for k in (0, 2):
                crossed.append(jnp.where(even, green[k], shift(green[k + 1], 1)))
                crossed.append(jnp.where(even, shift(green[k], -1), green[k + 1]))
            for r in range(2):
                left, right = crossed[r], crossed[r + 2]
                minus = -left
                tops = (
                    jnp.where(low_lane, left, shift(right, 2)),
                    jnp.where(low_lane, shift(left, -2), right),
                )
                bottoms = (
                    jnp.where(low_lane, right, shift(minus, 2)),
                    jnp.where(low_lane, shift(right, -2), minus),
                )
                for i in range(2):
                    out_ref[b, r + 2 * i, place, :] = tops[i].astype(bf16)
                    out_ref[b, r + 2 * i, below, :] = bottoms[i].astype(bf16)

    lax.fori_loop(0, blocks_here, one_block, 0)


def circle(cycles):
    x = cycles - jnp.round(cycles)
    z = x * x * (math.pi * math.pi)
    sine, cosine = 0.0, 0.0
    for n in range(5, -1, -1):
        sine = sine * z + (-1.0) ** n / math.factorial(2 * n + 1)
    for n in range(6, -1, -1):
        cosine = cosine * z + (-1.0) ** n / math.factorial(2 * n)
    sine = sine * x * math.pi
    return 1.0 - 2.0 * sine * sine, 2.0 * sine * cosine


def turn(a, b):
    return a[0] * b[0] - a[1] * b[1], a[0] * b[1] + a[1] * b[0]


def spectra_kernel(blocks_here, samples, first_step, onset_scale, slip_scale, live_ref, green_ref, *refs):
    steps = (len(refs) - 3) // 2
    packed, outs = refs[:steps][::-1], refs[steps : 2 * steps]
    waves, total, held = refs[-3:]
    variations, block_points = packed[0].shape[2:]
    bins = green_ref.shape[3]
    first_bin = (lax.axis_index("cmp") * bins).astype(f32)
    quarter = lax.broadcasted_iota(jnp.int32, (variations, bins), 1) // 4
    total[...] = jnp.zeros_like(total)
    for step in range(steps):
        held[step * blocks_here : (step + 1) * blocks_here] = packed[step][...]
    steps_per_word, words = live_words(first_step + steps, blocks_here)
    for word in range(words):
        flags = jnp.max(live_ref[word])
        low = max(first_step, word * steps_per_word)
        high = min(first_step + steps, (word + 1) * steps_per_word)

        def visit(place, carry):
            flag = jnp.right_shift(flags, place - word * steps_per_word * blocks_here) & 1

            @pl.when(flag == 1)
            def _():
                step = place // blocks_here
                local = place - step * blocks_here
                source = place - first_step * blocks_here
                onset = held[source, 0].astype(jnp.int32).astype(f32) + 32768.0
                slip = held[source, 1].astype(jnp.int32).astype(f32) * (1.0 / slip_scale)
                cycles = onset * (1.0 / (onset_scale * samples))
                one = circle(cycles)
                two = turn(one, one)
                four = turn(two, two)
                start = circle(cycles * first_bin)
                now = [(slip * start[0], slip * start[1])]
                now.append(turn(now[0], one))
                now.append(turn(now[0], two))
                now.append(turn(now[1], two))
                after = [turn(wave, four) for wave in now]
                double = 2.0 * four[0]
                for j in range(bins // 4):
                    rows = pl.ds(j * variations, variations)
                    for r in range(4):
                        waves[r, rows, 0:block_points] = now[r][0].astype(bf16)
                        waves[r, rows, block_points : 2 * block_points] = now[r][1].astype(bf16)
                    later = [
                        (double * after[r][0] - now[r][0], double * after[r][1] - now[r][1])
                        for r in range(4)
                    ]
                    now, after = after, later
                for r in range(4):
                    product = jnp.dot(waves[r], green_ref[local, r], preferred_element_type=f32)
                    found = product[0:variations]
                    for j in range(1, bins // 4):
                        found = jnp.where(
                            quarter == j, product[j * variations : (j + 1) * variations], found
                        )
                    total[step - first_step, r] += found

            return carry

        lax.fori_loop(low * blocks_here, high * blocks_here, visit, 0)
    for step in range(steps):
        outs[step][...] = total[step]


def spectra_call(first_step, onset_scale, slip_scale, live, green, received, name):
    steps = len(received)
    blocks_here, parts, variations, block_points = received[0].shape
    bins_here = green.shape[3]
    return pl.pallas_call(
        functools.partial(
            spectra_kernel, blocks_here, 4 * bins_here, first_step, onset_scale, slip_scale
        ),
        out_shape=[jax.ShapeDtypeStruct((4, variations, bins_here), f32)] * steps,
        in_specs=[VMEM] * (2 + steps),
        out_specs=[VMEM] * steps,
        scratch_shapes=[
            pltpu.VMEM((4, variations * bins_here // 4, 2 * block_points), bf16),
            pltpu.VMEM((steps, 4, variations, bins_here), f32),
            pltpu.VMEM((steps * blocks_here, parts, variations, block_points), jnp.int16),
        ],
        compiler_params=params(),
        cost_estimate=cost(steps * 1_000_000_000, 4_000_000 * steps),
        name=name,
    )(live, green, *received[::-1])


def three_products(left, table_high, table_low):
    rows = left.shape[0]
    coarse = left.astype(bf16)
    fine = (left - coarse.astype(f32)).astype(bf16)
    both = jnp.dot(
        jnp.concatenate([coarse, fine], axis=0), table_high, preferred_element_type=f32
    )
    return both[:rows] + both[rows:] + jnp.dot(coarse, table_low, preferred_element_type=f32)


def half_sign(bins, columns):
    odd = lax.broadcasted_iota(jnp.int32, (1, columns), 1) % bins % 2
    return (1 - 2 * odd * lax.axis_index("cmp")).astype(f32)


def band_kernel(
    bins, samples, row_ref, crossover_ref, high_ref, table_high, table_low, out_ref, weight_ref
):
    rows = jnp.concatenate([high_ref[0, :, c, :] for c in range(2)], axis=0)
    band = three_products(rows, table_high[...], table_low[...])
    sign = half_sign(bins, 2 * bins)
    out_ref[...] = -band * sign
    crossing = crossover_ref[row_ref[lax.axis_index("pt")]].astype(f32)
    column = lax.broadcasted_iota(jnp.int32, weight_ref.shape, 1) % bins
    taper = jnp.clip((crossing - column.astype(f32)) / taper_width + 0.5, 0.0, 1.0)
    weight_ref[...] = taper * (jnp.where(column == 0, 1.0, 2.0) / samples) * sign


def sum_kernel(bins_here, bins, band_ref, *refs):
    spectra, out_ref = refs[:-1], refs[-1]
    out_ref[...] = band_ref[...]
    half = lax.axis_index("cmp") * bins_here
    variations = spectra[0].shape[1]
    sums = []
    for r in range(4):
        piece = spectra[0][r]
        for other in spectra[1:]:
            piece = piece + other[r]
        sums.append(piece)
    lane = lax.broadcasted_iota(jnp.int32, (variations, bins_here), 1) % 4
    for k in range(4):
        spectrum = sums[0] if k == 0 else pltpu.roll(sums[0], bins_here - k, 1)
        for r in range(1, 4):
            moved = sums[r] if k == r else pltpu.roll(sums[r], (r - k) % bins_here, 1)
            spectrum = jnp.where(lane == r, moved, spectrum)
        place = pl.ds(pl.multiple_of((k // 2) * bins + half, bins_here), bins_here)
        rows = pl.ds((k % 2) * variations, variations)
        out_ref[rows, place] = out_ref[rows, place] + spectrum


def merge_kernel(own_ref, other_ref, weight_ref, high_ref, table_high, table_low, out_ref):
    excess = (own_ref[...] + other_ref[...]) * weight_ref[0:1]
    low = three_products(excess, table_high[...], table_low[...])
    variations = high_ref.shape[1]
    for c in range(2):
        out_ref[0, :, c, :] = high_ref[0, :, c, :] + low[c * variations : (c + 1) * variations]


def body(
    pt_size,
    strain_green,
    green_scale,
    mechanism,
    slip_amplitude,
    onset_time,
    rupture_row,
    rupture_blocks,
    block_count,
    crossover,
    high_band,
):
    points_here, strain_rows, bins_here = strain_green.shape
    blocks_here = green_scale.shape[0]
    block_points = points_here // blocks_here
    variations = slip_amplitude.shape[1]
    samples_here = high_band.shape[3]
    halves = 2
    bins = halves * bins_here
    samples = halves * samples_here
    assert slip_amplitude.shape[0] == 1 and pt_size & (pt_size - 1) == 0
    assert samples == 2 * bins and strain_rows == 24

    strain_lines = strain_green.reshape(points_here * strain_rows, bins_here)
    head_blocks = 1
    head_shape = jax.ShapeDtypeStruct((head_blocks * block_points * strain_rows, bins_here), bf16)
    pack_shape = jax.ShapeDtypeStruct((blocks_here, 2, variations, block_points), jnp.int16)
    live_shape = jax.ShapeDtypeStruct((live_words(pt_size, blocks_here)[1], 8, 128), jnp.int32)
    onset_scale, slip_scale = 512.0, 1024.0
    *packed, live, head = pl.pallas_call(
        functools.partial(pack_kernel, blocks_here, block_points, onset_scale, slip_scale),
        out_shape=[pack_shape] * pt_size + [live_shape, head_shape],
        in_specs=[HBM] * 6,
        out_specs=[VMEM] * (pt_size + 2),
        scratch_shapes=scalar_scratch((rupture_row, rupture_blocks, block_count))
        + [pltpu.VMEM(a.shape, a.dtype) for a in (slip_amplitude, onset_time)]
        + [pltpu.SemaphoreType.DMA((5,)), pltpu.SemaphoreType.DMA],
        compiler_params=params(),
        name="pack",
    )(
        *in_hbm(
            rupture_row, rupture_blocks, block_count, slip_amplitude, onset_time, strain_lines
        )
    )

    def swap(value, step):
        return lax.ppermute(value, "pt", [(i, i ^ step) for i in range(pt_size)])

    def exchange(values):
        moved = [swap(values[step], step) for step in range(pt_size - 1, 0, -1)]
        return [values[0]] + moved[::-1]

    received = exchange(packed)

    green = pl.pallas_call(
        functools.partial(green_kernel, pt_size),
        out_shape=jax.ShapeDtypeStruct((blocks_here, 4, 2 * block_points, bins_here), bf16),
        in_specs=[VMEM] * 2 + [HBM] * 3,
        out_specs=VMEM,
        scratch_shapes=[
            pltpu.VMEM((blocks_here, block_points * strain_rows + 64, bins_here), bf16),
            pltpu.VMEM((points_here, 8 * strain_rows + 64), f32),
            pltpu.VMEM(green_scale.shape, f32),
            pltpu.VMEM(mechanism.shape, f32),
            pltpu.SemaphoreType.DMA((blocks_here,)),
            pltpu.SemaphoreType.DMA((2,)),
        ],
        compiler_params=params(),
        cost_estimate=cost(2 * points_here * strain_rows * bins_here, 6_000_000),
        name="green",
    )(live, head, *in_hbm(strain_lines, green_scale, mechanism))

    sent = spectra_call(1, onset_scale, slip_scale, live, green, received[1:], "spectra")
    gathered = exchange([None] + list(sent))
    gathered[0], = spectra_call(0, onset_scale, slip_scale, live, green, received[:1], "own")

    table = fourier_table(bins, samples, samples_here)
    table_high, table_low = split_table(table)
    turned_high, turned_low = split_table(np.ascontiguousarray(table.T))
    rows = 2 * variations
    band, weight = pl.pallas_call(
        functools.partial(band_kernel, bins, samples),
        out_shape=[
            jax.ShapeDtypeStruct((rows, 2 * bins), f32),
            jax.ShapeDtypeStruct((8, 2 * bins), f32),
        ],
        in_specs=[SMEM] * 2 + [VMEM] * 3,
        out_specs=[VMEM] * 2,
        compiler_params=params(),
        cost_estimate=cost(6 * rows * samples_here * 2 * bins, 1_000_000),
        name="band",
    )(rupture_row, crossover, high_band, jnp.asarray(turned_high), jnp.asarray(turned_low))

    excess = pl.pallas_call(
        functools.partial(sum_kernel, bins_here, bins),
        out_shape=jax.ShapeDtypeStruct((rows, 2 * bins), f32),
        in_specs=[VMEM] * (1 + pt_size),
        out_specs=VMEM,
        compiler_params=params(),
        name="excess",
    )(band, *gathered[::-1])
    other = lax.ppermute(excess, "cmp", [(0, 1), (1, 0)])

    return pl.pallas_call(
        merge_kernel,
        out_shape=jax.ShapeDtypeStruct(high_band.shape, f32),
        in_specs=[VMEM] * 6,
        out_specs=VMEM,
        compiler_params=params(),
        name="merge",
    )(excess, other, weight, high_band, jnp.asarray(table_high), jnp.asarray(table_low))


def solution(mesh):
    assert mesh.shape["cmp"] == 2
    return jax.shard_map(
        functools.partial(body, mesh.shape["pt"]),
        mesh=mesh,
        in_specs=(
            P(("site", "pt"), None, "cmp"),
            P(("site", "pt"), None),
            P(None, "pt"),
            P("pt", "var", None),
            P("pt", "var", None),
            P(),
            P(),
            P(),
            P(),
            P(("site", "pt"), "var", None, "cmp"),
        ),
        out_specs=P(("site", "pt"), "var", None, "cmp"),
        check_vma=False,
    )
```

profile of v0, /device:TPU:0, one launch (start us, length us, event | category | flops | bytes accessed | tf_op | source)
XLA Modules:
  0.0 23.2 jit_solution(2346716504760024432)
XLA Ops:
  0.0 1.3 %pack.1 = (s16[5,2,16,128]{3,2,1,0:T(8,128)(2,1)S(1)}, s16[5,2,16,128]{3,2,1,0:T(8,128)(2,1)S(1)}, s16[5,2,16,128]{3,2,1,0:T(8,128)(2,1)S(1)}, s16[5,2,16,128]{3...) custom-call(s32[4]{0:T(128)} %refs_0_.1, s32[4,12]{1,0:T(4,128)} %refs_1_.1, s32[4]{0:T(128)} %refs_2_.1, ...), custom_call_target="tpu_custom_call" | custom-call | tf_op jit(solution)/shard_map/pack/pallas_call | solution.py:434
  1.3 5.1 %collective-permute-start = (s16[5,2,16,128]{3,2,1,0:T(8,128)(2,1)S(1)}, s16[5,2,16,128]{3,2,1,0:T(8,128)(2,1)S(1)}, u32[]{:S(2)}, u32[]{:S(2)}) collective-permute-start(s16[5,2,16,128]{3,2,1,0:T(8,128)(2,1)S(1)} %get-tuple-element.19), channel_id=1, source_target_pairs={{0,12},{4,8},{8,4},{12,0},{1,13},{5,9},{9,5},{13,1},{2,14},{6,10},... | collective-permute-start | bytes 122888 | tf_op jit(solution)/shard_map/ppermute | solution.py:451
  6.4 0.0 collective-permute-start.1
  6.4 0.6 %collective-permute-start.2 = (s16[5,2,16,128]{3,2,1,0:T(8,128)(2,1)S(1)}, s16[5,2,16,128]{3,2,1,0:T(8,128)(2,1)S(1)}, u32[]{:S(2)}, u32[]{:S(2)}) collective-permute-start(s16[5,2,16,128]{3,2,1,0:T(8,128)(2,1)S(1)} %get-tuple-element.21), channel_id=1, source_target_pairs={{0,4},{4,0},{8,12},{12,8},{1,5},{5,1},{9,13},{13,9},{2,6},{6,2},{1... | collective-permute-start | bytes 122888 | tf_op jit(solution)/shard_map/ppermute | solution.py:451
  7.0 2.6 %green.1.green_ref = bf16[5,4,256,128]{3,2,1,0:T(8,128)(2,1)S(1)} custom-call(s32[1,8,128]{2,1,0:T(8,128)S(1)} %get-tuple-element.17.live_ref, bf16[3072,128]{1,0:T(8,128)(2,1)S(1)} %get-tuple-element.18.head_ref, bf16[15360,128]{1,0:T(8,128)(2,1)} %bitcast.2, f32[5,24]{1,0:T(8,128)} %scale_hbm.1, f32[6,640]{1,0:T(8,128)} %mechanism_hbm.1), custom_call_target="tpu_custom_call" | custom-call | flops 3932160 | bytes 6000000 | tf_op jit(solution)/shard_map/green/pallas_call | solution.py:459
  9.7 0.0 copy-start.2
  9.7 0.0 copy-start.3
  9.7 0.0 copy-start.4
  9.7 0.0 copy-start.5
  9.7 0.0 copy-start.6
  9.7 1.6 %collective-permute-done.1.refs_1_ = s16[5,2,16,128]{3,2,1,0:T(8,128)(2,1)S(1)} collective-permute-done((s16[5,2,16,128]{3,2,1,0:T(8,128)(2,1)S(1)}, s16[5,2,16,128]{3,2,1,0:T(8,128)(2,1)S(1)}, u32[]{:S(2)}, u32[]{:S(2)}) %collective-permute-start.1) | collective-permute-done | bytes 40992 | tf_op jit(solution)/shard_map/ppermute | solution.py:451
  11.3 1.7 %spectra.1 = (f32[4,16,128]{2,1,0:T(8,128)S(1)}, f32[4,16,128]{2,1,0:T(8,128)S(1)}, f32[4,16,128]{2,1,0:T(8,128)S(1)}) custom-call(s32[1,8,128]{2,1,0:T(8,128)S(1)} %get-tuple-element.17.live_ref, bf16[5,4,256,128]{3,2,1,0:T(8,128)(2,1)S(1)} %green.1.green_ref, s16[5,2,16,128]{3,2,1,0:T(8,128)(2,1)S(1)} %collective-permute-done.refs_0_, ...), custom_call_target="tpu_custom_call" | custom-call | flops 3000000000 | bytes 12000000 | tf_op jit(solution)/shard_map/spectra/pallas_call | solution.py:328
  13.0 0.0 copy-start
  13.0 0.0 copy-start.1
  13.0 3.1 %collective-permute-start.3 = (f32[4,16,128]{2,1,0:T(8,128)S(1)}, f32[4,16,128]{2,1,0:T(8,128)S(1)}, u32[]{:S(2)}, u32[]{:S(2)}) collective-permute-start(f32[4,16,128]{2,1,0:T(8,128)S(1)} %get-tuple-element.22), channel_id=1, source_target_pairs={{0,12},{4,8},{8,4},{12,0},{1,13},{5,9},{9,5},{13,1},{2,14},{6,10},... | collective-permute-start | bytes 98312 | tf_op jit(solution)/shard_map/ppermute | solution.py:451
  16.1 1.4 %collective-permute-start.5 = (f32[4,16,128]{2,1,0:T(8,128)S(1)}, f32[4,16,128]{2,1,0:T(8,128)S(1)}, u32[]{:S(2)}, u32[]{:S(2)}) collective-permute-start(f32[4,16,128]{2,1,0:T(8,128)S(1)} %get-tuple-element.24), channel_id=1, source_target_pairs={{0,4},{4,0},{8,12},{12,8},{1,5},{5,1},{9,13},{13,9},{2,6},{6,2},{1... | collective-permute-start | bytes 98312 | tf_op jit(solution)/shard_map/ppermute | solution.py:451
  17.5 0.3 %own.1.refs_3_ = f32[4,16,128]{2,1,0:T(8,128)S(1)} custom-call(s32[1,8,128]{2,1,0:T(8,128)S(1)} %get-tuple-element.17.live_ref, bf16[5,4,256,128]{3,2,1,0:T(8,128)(2,1)S(1)} %green.1.green_ref, s16[5,2,16,128]{3,2,1,0:T(8,128)(2,1)S(1)} %get-tuple-element.25.refs_0_), custom_call_target="tpu_custom_call" | custom-call | flops 1000000000 | bytes 4000000 | tf_op jit(solution)/shard_map/own/pallas_call | solution.py:328
  17.8 0.7 %band.1 = (f32[32,512]{1,0:T(8,128)S(1)}, f32[8,512]{1,0:T(8,128)S(1)}) custom-call(s32[4]{0:T(128)S(1)} %copy-done.5, s32[4]{0:T(128)S(1)} %copy-done.6, f32[1,16,2,256]{3,2,1,0:T(2,128)S(1)} %copy-done.4, bf16[256,512]{1,0:T(8,128)(2,1)S(1)} %copy-done.2, bf16[256,512]{1,0:T(8,128)(2,1)S(1)} %copy-done.3), custom_call_target="tpu_custom_call" | custom-call | flops 25165824 | bytes 1000000 | tf_op jit(solution)/shard_map/band/pallas_call | solution.py:485
  18.6 0.4 %collective-permute-done.3.refs_0_ = f32[4,16,128]{2,1,0:T(8,128)S(1)} collective-permute-done((f32[4,16,128]{2,1,0:T(8,128)S(1)}, f32[4,16,128]{2,1,0:T(8,128)S(1)}, u32[]{:S(2)}, u32[]{:S(2)}) %collective-permute-start.3) | collective-permute-done | bytes 32800 | tf_op jit(solution)/shard_map/ppermute | solution.py:451
  18.9 2.0 %collective-permute-done.4.refs_1_ = f32[4,16,128]{2,1,0:T(8,128)S(1)} collective-permute-done((f32[4,16,128]{2,1,0:T(8,128)S(1)}, f32[4,16,128]{2,1,0:T(8,128)S(1)}, u32[]{:S(2)}, u32[]{:S(2)}) %collective-permute-start.4) | collective-permute-done | bytes 32800 | tf_op jit(solution)/shard_map/ppermute | solution.py:451
  21.0 0.1 excess.1.own_ref
  21.1 0.1 collective-permute-start.6
  21.1 1.2 %collective-permute-done.6.other_ref = f32[32,512]{1,0:T(8,128)S(1)} collective-permute-done((f32[32,512]{1,0:T(8,128)S(1)}, f32[32,512]{1,0:T(8,128)S(1)}, u32[]{:S(2)}, u32[]{:S(2)}) %collective-permute-start.6) | collective-permute-done | bytes 65568 | tf_op jit(solution)/shard_map/ppermute | solution.py:506
  22.4 0.8 %merge.1 = f32[1,16,2,256]{3,2,1,0:T(2,128)} custom-call(f32[32,512]{1,0:T(8,128)S(1)} %excess.1.own_ref, f32[32,512]{1,0:T(8,128)S(1)} %collective-permute-done.6.other_ref, f32[8,512]{1,0:T(8,128)S(1)} %get-tuple-element.26.weight_ref, f32[1,16,2,256]{3,2,1,0:T(2,128)S(1)} %copy-done.4, bf16[512,256]{1,0:T(8,128)(2,1)S(1)} %copy-done, ...), custom_call_target="tpu_custom_call" | custom-call | tf_op jit(solution)/shard_map/merge/pallas_call | solution.py:508
  (11 shorter events, 0.0 us)
Async XLA Ops:
  1.3 8.5 %collective-permute-start = (s16[5,2,16,128]{3,2,1,0:T(8,128)(2,1)S(1)}, s16[5,2,16,128]{3,2,1,0:T(8,128)(2,1)S(1)}, u32[]{:S(2)}, u32[]{:S(2)}) collective-permute-start(s16[5,2,16,128]{3,2,1,0:T(8,128)(2,1)S(1)} %get-tuple-element.19), channel_id=1, source_target_pairs={{0,12},{4,8},{8,4},{12,0},{1,13},{5,9},{9,5},{13,1},{2,14},{6,10},... | collective-permute-start | bytes 122888 | tf_op jit(solution)/shard_map/ppermute | solution.py:451
  6.4 4.9 %collective-permute-start.1 = (s16[5,2,16,128]{3,2,1,0:T(8,128)(2,1)S(1)}, s16[5,2,16,128]{3,2,1,0:T(8,128)(2,1)S(1)}, u32[]{:S(2)}, u32[]{:S(2)}) collective-permute-start(s16[5,2,16,128]{3,2,1,0:T(8,128)(2,1)S(1)} %get-tuple-element.20), channel_id=1, source_target_pairs={{0,8},{4,12},{8,0},{12,4},{1,9},{5,13},{9,1},{13,5},{2,10},{6,14},... | collective-permute-start | bytes 122888 | tf_op jit(solution)/shard_map/ppermute | solution.py:451
  6.4 4.9 %collective-permute-start.2 = (s16[5,2,16,128]{3,2,1,0:T(8,128)(2,1)S(1)}, s16[5,2,16,128]{3,2,1,0:T(8,128)(2,1)S(1)}, u32[]{:S(2)}, u32[]{:S(2)}) collective-permute-start(s16[5,2,16,128]{3,2,1,0:T(8,128)(2,1)S(1)} %get-tuple-element.21), channel_id=1, source_target_pairs={{0,4},{4,0},{8,12},{12,8},{1,5},{5,1},{9,13},{13,9},{2,6},{6,2},{1... | collective-permute-start | bytes 122888 | tf_op jit(solution)/shard_map/ppermute | solution.py:451
  9.7 8.1 %copy-start.2 = (bf16[256,512]{1,0:T(8,128)(2,1)S(1)}, bf16[256,512]{1,0:T(8,128)(2,1)}, u32[]{:S(2)}) copy-start(bf16[256,512]{1,0:T(8,128)(2,1)} %constant.8.clone.table_high) | copy-start | bytes 786436
  9.7 8.1 %copy-start.3 = (bf16[256,512]{1,0:T(8,128)(2,1)S(1)}, bf16[256,512]{1,0:T(8,128)(2,1)}, u32[]{:S(2)}) copy-start(bf16[256,512]{1,0:T(8,128)(2,1)} %constant.9.clone.table_low) | copy-start | bytes 786436
  9.7 8.1 %copy-start.4 = (f32[1,16,2,256]{3,2,1,0:T(2,128)S(1)}, f32[1,16,2,256]{3,2,1,0:T(2,128)}, u32[]{:S(2)}) copy-start(f32[1,16,2,256]{3,2,1,0:T(2,128)} %high_ref.3) | copy-start | bytes 98308
  9.7 8.1 %copy-start.5 = (s32[4]{0:T(128)S(1)}, s32[4]{0:T(128)}, u32[]{:S(2)}) copy-start(s32[4]{0:T(128)} %refs_0_.1) | copy-start | bytes 52
  9.7 8.1 %copy-start.6 = (s32[4]{0:T(128)S(1)}, s32[4]{0:T(128)}, u32[]{:S(2)}) copy-start(s32[4]{0:T(128)} %crossover_ref.1) | copy-start | bytes 52
  13.0 9.4 %copy-start = (bf16[512,256]{1,0:T(8,128)(2,1)S(1)}, bf16[512,256]{1,0:T(8,128)(2,1)}, u32[]{:S(2)}) copy-start(bf16[512,256]{1,0:T(8,128)(2,1)} %constant.10.clone.table_high) | copy-start | bytes 786436
  13.0 9.4 %copy-start.1 = (bf16[512,256]{1,0:T(8,128)(2,1)S(1)}, bf16[512,256]{1,0:T(8,128)(2,1)}, u32[]{:S(2)}) copy-start(bf16[512,256]{1,0:T(8,128)(2,1)} %constant.11.clone.table_low) | copy-start | bytes 786436
  13.0 5.9 %collective-permute-start.3 = (f32[4,16,128]{2,1,0:T(8,128)S(1)}, f32[4,16,128]{2,1,0:T(8,128)S(1)}, u32[]{:S(2)}, u32[]{:S(2)}) collective-permute-start(f32[4,16,128]{2,1,0:T(8,128)S(1)} %get-tuple-element.22), channel_id=1, source_target_pairs={{0,12},{4,8},{8,4},{12,0},{1,13},{5,9},{9,5},{13,1},{2,14},{6,10},... | collective-permute-start | bytes 98312 | tf_op jit(solution)/shard_map/ppermute | solution.py:451
  16.1 4.8 %collective-permute-start.4 = (f32[4,16,128]{2,1,0:T(8,128)S(1)}, f32[4,16,128]{2,1,0:T(8,128)S(1)}, u32[]{:S(2)}, u32[]{:S(2)}) collective-permute-start(f32[4,16,128]{2,1,0:T(8,128)S(1)} %get-tuple-element.23), channel_id=1, source_target_pairs={{0,8},{4,12},{8,0},{12,4},{1,9},{5,13},{9,1},{13,5},{2,10},{6,14},... | collective-permute-start | bytes 98312 | tf_op jit(solution)/shard_map/ppermute | solution.py:451
  16.1 4.8 %collective-permute-start.5 = (f32[4,16,128]{2,1,0:T(8,128)S(1)}, f32[4,16,128]{2,1,0:T(8,128)S(1)}, u32[]{:S(2)}, u32[]{:S(2)}) collective-permute-start(f32[4,16,128]{2,1,0:T(8,128)S(1)} %get-tuple-element.24), channel_id=1, source_target_pairs={{0,4},{4,0},{8,12},{12,8},{1,5},{5,1},{9,13},{13,9},{2,6},{6,2},{1... | collective-permute-start | bytes 98312 | tf_op jit(solution)/shard_map/ppermute | solution.py:451
  21.1 1.3 %collective-permute-start.6 = (f32[32,512]{1,0:T(8,128)S(1)}, f32[32,512]{1,0:T(8,128)S(1)}, u32[]{:S(2)}, u32[]{:S(2)}) collective-permute-start(f32[32,512]{1,0:T(8,128)S(1)} %excess.1.own_ref), channel_id=1, source_target_pairs={{0,1},{1,0},{2,3},{3,2},{4,5},{5,4},{6,7},{7,6},{8,9},{9,8},{10,11... | collective-permute-start | bytes 196616 | tf_op jit(solution)/shard_map/ppermute | solution.py:506
where the time goes:
time: 23.2 us
  starting transfers between devices  10.3 us (44%)
  Pallas kernels  7.52 us (32%)
  waiting for transfers between devices  5.2 us (22%)
    ppermute x6, starting transfers between devices, swap(): return lax.ppermute(value, 'pt', [(i, i ^ step) for i in range(pt_size)])  10.2 us
    ppermute x6, waiting for transfers between devices, swap(): return lax.ppermute(value, 'pt', [(i, i ^ step) for i in range(pt_size)])  3.96 us
    pallas_call x1, Pallas kernels, body(): pl.pallas_call(functools.partial(green_kernel, pt_size), out_shape=jax.Sh...  2.63 us
    pallas_call x2, Pallas kernels, spectra_call(): pl.pallas_call(functools.partial(spectra_kernel, blocks_here, 4 * bins_he...  1.97 us
    pallas_call x1, Pallas kernels, body(): pl.pallas_call(functools.partial(pack_kernel, blocks_here, block_points,...  1.27 us
    ppermute x1, waiting for transfers between devices, body(): other = lax.ppermute(excess, 'cmp', [(0, 1), (1, 0)])  1.24 us
    pallas_call x1, Pallas kernels, body(): pl.pallas_call(merge_kernel, out_shape=jax.ShapeDtypeStruct(high_band.sha...  0.83 us
    pallas_call x1, Pallas kernels, body(): pl.pallas_call(functools.partial(band_kernel, bins, samples), out_shape=[...  0.74 us
  transfers between devices with their start and end apart: 7, of which 4 were waited for; matrix products, arithmetic and copies ran while one was open for 0% of the time, Pallas kernels for 16%

commit v1 on v0

--- a/solution.py
+++ b/solution.py
@@ -64,12 +64,15 @@
 
 
 def pack_kernel(blocks_here, block_points, onset_scale, slip_scale, *refs):
-    sources, strain_hbm, outs = refs[:5], refs[5], refs[6:-9]
-    live_ref, head_ref, targets, sems, head_sem = refs[-9], refs[-8], refs[-7:-2], refs[-2], refs[-1]
+    sources, later_sources, strain_hbm, outs = refs[:5], refs[5:7], refs[7], refs[8:-12]
+    live_ref, head_ref, later_targets = refs[-12], refs[-11], refs[-10:-8]
+    targets, sems, later_sems, head_sem = refs[-8:-3], refs[-3], refs[-2], refs[-1]
     row_ref, blocks_ref, count_ref, slip_ref, onset_ref = targets
     copies = fetch(sources, targets, sems)
+    later = fetch(later_sources, later_targets, later_sems)
     head = pltpu.make_async_copy(strain_hbm.at[pl.ds(0, head_ref.shape[0])], head_ref, head_sem)
     head.start()
+    later.append(head)
     for copy in copies[:3]:
         copy.wait()
     me = lax.axis_index("pt")
@@ -112,7 +115,8 @@
         return carry
 
     lax.fori_loop(0, count_ref[rupture], visit, 0)
-    head.wait()
+    for copy in later:
+        copy.wait()
 
 
 def three_parts(values):
@@ -124,9 +128,8 @@
 
 
 def green_kernel(
-    steps, live_ref, head_ref, strain_hbm, scale_hbm, mechanism_hbm, out_ref, strain_ref, factor_ref, scale_ref, mechanism_ref, sems, small_sems
+    steps, live_ref, head_ref, strain_hbm, scale_ref, mechanism_ref, out_ref, strain_ref, factor_ref, sems
 ):
-    small = fetch((scale_hbm, mechanism_hbm), (scale_ref, mechanism_ref), small_sems)
     rows, octet = 24, 8
     wide, depth = octet * rows, factor_ref.shape[1]
     blocks_here = scale_ref.shape[0]
@@ -143,8 +146,6 @@
         strain_copy(b, head_ref if b * per_block < head_ref.shape[0] else strain_hbm).start()
     for b in range(blocks_here):
         strain_ref[b, per_block:, :] = jnp.zeros((depth - wide, bins), bf16)
-    for copy in small:
-        copy.wait()
     column = lax.broadcasted_iota(jnp.int32, (18, depth), 1) % rows
     spread_six = column % 6 == lax.broadcasted_iota(jnp.int32, (18, depth), 0) % 6
     column = lax.broadcasted_iota(jnp.int32, (3 * rows, depth), 1) % rows
@@ -257,17 +258,21 @@
     return a[0] * b[0] - a[1] * b[1], a[0] * b[1] + a[1] * b[0]
 
 
+def arrival_order(first_step, steps):
+    return sorted(range(steps), key=lambda step: -((first_step + step) & -2))
+
+
 def spectra_kernel(blocks_here, samples, first_step, onset_scale, slip_scale, live_ref, green_ref, *refs):
     steps = (len(refs) - 3) // 2
-    packed, outs = refs[:steps][::-1], refs[steps : 2 * steps]
+    packed, outs = refs[:steps], refs[steps : 2 * steps]
     waves, total, held = refs[-3:]
     variations, block_points = packed[0].shape[2:]
     bins = green_ref.shape[3]
     first_bin = (lax.axis_index("cmp") * bins).astype(f32)
     quarter = lax.broadcasted_iota(jnp.int32, (variations, bins), 1) // 4
     total[...] = jnp.zeros_like(total)
-    for step in range(steps):
-        held[step * blocks_here : (step + 1) * blocks_here] = packed[step][...]
+    for place, step in enumerate(arrival_order(first_step, steps)):
+        held[step * blocks_here : (step + 1) * blocks_here] = packed[place][...]
     steps_per_word, words = live_words(first_step + steps, blocks_here)
     for word in range(words):
         flags = jnp.max(live_ref[word])
@@ -340,7 +345,7 @@
         compiler_params=params(),
         cost_estimate=cost(steps * 1_000_000_000, 4_000_000 * steps),
         name=name,
-    )(live, green, *received[::-1])
+    )(live, green, *[received[step] for step in arrival_order(first_step, steps)])
 
 
 def three_products(left, table_high, table_low):
@@ -431,19 +436,32 @@
     pack_shape = jax.ShapeDtypeStruct((blocks_here, 2, variations, block_points), jnp.int16)
     live_shape = jax.ShapeDtypeStruct((live_words(pt_size, blocks_here)[1], 8, 128), jnp.int32)
     onset_scale, slip_scale = 512.0, 1024.0
-    *packed, live, head = pl.pallas_call(
+    *packed, live, head, scale_here, mechanism_here = pl.pallas_call(
         functools.partial(pack_kernel, blocks_here, block_points, onset_scale, slip_scale),
-        out_shape=[pack_shape] * pt_size + [live_shape, head_shape],
-        in_specs=[HBM] * 6,
-        out_specs=[VMEM] * (pt_size + 2),
+        out_shape=[pack_shape] * pt_size
+        + [live_shape, head_shape]
+        + [jax.ShapeDtypeStruct(a.shape, a.dtype) for a in (green_scale, mechanism)],
+        in_specs=[HBM] * 8,
+        out_specs=[VMEM] * (pt_size + 4),
         scratch_shapes=scalar_scratch((rupture_row, rupture_blocks, block_count))
         + [pltpu.VMEM(a.shape, a.dtype) for a in (slip_amplitude, onset_time)]
-        + [pltpu.SemaphoreType.DMA((5,)), pltpu.SemaphoreType.DMA],
+        + [
+            pltpu.SemaphoreType.DMA((5,)),
+            pltpu.SemaphoreType.DMA((2,)),
+            pltpu.SemaphoreType.DMA,
+        ],
         compiler_params=params(),
         name="pack",
     )(
         *in_hbm(
-            rupture_row, rupture_blocks, block_count, slip_amplitude, onset_time, strain_lines
+            rupture_row,
+            rupture_blocks,
+            block_count,
+            slip_amplitude,
+            onset_time,
+            green_scale,
+            mechanism,
+            strain_lines,
         )
     )
 
@@ -459,20 +477,17 @@
     green = pl.pallas_call(
         functools.partial(green_kernel, pt_size),
         out_shape=jax.ShapeDtypeStruct((blocks_here, 4, 2 * block_points, bins_here), bf16),
-        in_specs=[VMEM] * 2 + [HBM] * 3,
+        in_specs=[VMEM] * 2 + [HBM] + [VMEM] * 2,
         out_specs=VMEM,
         scratch_shapes=[
             pltpu.VMEM((blocks_here, block_points * strain_rows + 64, bins_here), bf16),
             pltpu.VMEM((points_here, 8 * strain_rows + 64), f32),
-            pltpu.VMEM(green_scale.shape, f32),
-            pltpu.VMEM(mechanism.shape, f32),
             pltpu.SemaphoreType.DMA((blocks_here,)),
-            pltpu.SemaphoreType.DMA((2,)),
         ],
         compiler_params=params(),
         cost_estimate=cost(2 * points_here * strain_rows * bins_here, 6_000_000),
         name="green",
-    )(live, head, *in_hbm(strain_lines, green_scale, mechanism))
+    )(live, head, *in_hbm(strain_lines), scale_here, mechanism_here)
 
     sent = spectra_call(1, onset_scale, slip_scale, live, green, received[1:], "spectra")
     gathered = exchange([None] + list(sent))

time: 23.2 us -> 22.5 us (0.970)
  Pallas kernels: 7.52 us -> 7.1 us
    pallas_call x2, Pallas kernels: 1.97 us -> 1.52 us  [spectra_call(): pl.pallas_call(functools.partial(spectra_kernel, blocks_here, 4 * bins_he...]
    pallas_call x1, Pallas kernels: 1.27 us -> 1.51 us  [body(): pl.pallas_call(functools.partial(pack_kernel, blocks_here, block_points,...]
  transfers between devices with their start and end apart: 7 -> 7, of which waited for: 4 -> 4; matrix products, arithmetic and copies ran while one was open for 0% -> 0% of each run, Pallas kernels for 16% -> 19%
where the time goes in v1:
time: 22.5 us; the launch traced here: 22.6 us
  starting transfers between devices  10.1 us (45%)
  Pallas kernels  7.1 us (32%)
  waiting for transfers between devices  5.22 us (23%)
    ppermute x6, starting transfers between devices, swap(): return lax.ppermute(value, 'pt', [(i, i ^ step) for i in range(pt_size)])  9.99 us
    ppermute x6, waiting for transfers between devices, swap(): return lax.ppermute(value, 'pt', [(i, i ^ step) for i in range(pt_size)])  3.98 us
    pallas_call x1, Pallas kernels, body(): pl.pallas_call(functools.partial(green_kernel, pt_size), out_shape=jax.Sh...  2.41 us
    pallas_call x2, Pallas kernels, spectra_call(): pl.pallas_call(functools.partial(spectra_kernel, blocks_here, 4 * bins_he...  1.52 us
    pallas_call x1, Pallas kernels, body(): pl.pallas_call(functools.partial(pack_kernel, blocks_here, block_points,...  1.51 us
    ppermute x1, waiting for transfers between devices, body(): other = lax.ppermute(excess, 'cmp', [(0, 1), (1, 0)])  1.24 us
    pallas_call x1, Pallas kernels, body(): pl.pallas_call(merge_kernel, out_shape=jax.ShapeDtypeStruct(high_band.sha...  0.83 us
    pallas_call x1, Pallas kernels, body(): pl.pallas_call(functools.partial(band_kernel, bins, samples), out_shape=[...  0.74 us
  transfers between devices with their start and end apart: 7, of which 4 were waited for; matrix products, arithmetic and copies ran while one was open for 0% of the time, Pallas kernels for 19%

profile of v1, /device:TPU:0, one launch (start us, length us, event | category | flops | bytes accessed | tf_op | source)
XLA Modules:
  0.0 22.6 jit_solution(4927073537261589424)
XLA Ops:
  0.0 1.5 %pack.1 = (s16[5,2,16,128]{3,2,1,0:T(8,128)(2,1)S(1)}, s16[5,2,16,128]{3,2,1,0:T(8,128)(2,1)S(1)}, s16[5,2,16,128]{3,2,1,0:T(8,128)(2,1)S(1)}, s16[5,2,16,128]{3...) custom-call(s32[4]{0:T(128)} %refs_0_.1, ...), custom_call_target="tpu_custom_call" | custom-call | tf_op jit(solution)/shard_map/pack/pallas_call | solution.py:439
  1.5 3.9 %collective-permute-start = (s16[5,2,16,128]{3,2,1,0:T(8,128)(2,1)S(1)}, s16[5,2,16,128]{3,2,1,0:T(8,128)(2,1)S(1)}, u32[]{:S(2)}, u32[]{:S(2)}) collective-permute-start(s16[5,2,16,128]{3,2,1,0:T(8,128)(2,1)S(1)} %get-tuple-element.23), channel_id=1, source_target_pairs={{0,8},{4,12},{8,0},{12,4},{1,9},{5,13},{9,1},{13,5},{2,10},{6,14},... | collective-permute-start | bytes 122888 | tf_op jit(solution)/shard_map/ppermute | solution.py:469
  5.4 1.3 %collective-permute-start.1 = (s16[5,2,16,128]{3,2,1,0:T(8,128)(2,1)S(1)}, s16[5,2,16,128]{3,2,1,0:T(8,128)(2,1)S(1)}, u32[]{:S(2)}, u32[]{:S(2)}) collective-permute-start(s16[5,2,16,128]{3,2,1,0:T(8,128)(2,1)S(1)} %get-tuple-element.24), channel_id=1, source_target_pairs={{0,12},{4,8},{8,4},{12,0},{1,13},{5,9},{9,5},{13,1},{2,14},{6,10},... | collective-permute-start | bytes 122888 | tf_op jit(solution)/shard_map/ppermute | solution.py:469
  6.8 0.2 %collective-permute-start.2 = (s16[5,2,16,128]{3,2,1,0:T(8,128)(2,1)S(1)}, s16[5,2,16,128]{3,2,1,0:T(8,128)(2,1)S(1)}, u32[]{:S(2)}, u32[]{:S(2)}) collective-permute-start(s16[5,2,16,128]{3,2,1,0:T(8,128)(2,1)S(1)} %get-tuple-element.25), channel_id=1, source_target_pairs={{0,4},{4,0},{8,12},{12,8},{1,5},{5,1},{9,13},{13,9},{2,6},{6,2},{1... | collective-permute-start | bytes 122888 | tf_op jit(solution)/shard_map/ppermute | solution.py:469
  7.0 2.4 %green.1.green_ref = bf16[5,4,256,128]{3,2,1,0:T(8,128)(2,1)S(1)} custom-call(s32[1,8,128]{2,1,0:T(8,128)S(1)} %get-tuple-element.19.live_ref, bf16[3072,128]{1,0:T(8,128)(2,1)S(1)} %get-tuple-element.20.head_ref, bf16[15360,128]{1,0:T(8,128)(2,1)} %bitcast.2, f32[5,24]{1,0:T(8,128)S(1)} %get-tuple-element.21.scale_ref, ...), custom_call_target="tpu_custom_call" | custom-call | flops 3932160 | bytes 6000000 | tf_op jit(solution)/shard_map/green/pallas_call | solution.py:477
  9.4 0.0 copy-start.2
  9.4 0.0 copy-start.3
  9.5 0.0 copy-start.4
  9.5 0.0 copy-start.5
  9.5 0.0 copy-start.6
  9.5 1.7 %collective-permute-done.1.refs_1_ = s16[5,2,16,128]{3,2,1,0:T(8,128)(2,1)S(1)} collective-permute-done((s16[5,2,16,128]{3,2,1,0:T(8,128)(2,1)S(1)}, s16[5,2,16,128]{3,2,1,0:T(8,128)(2,1)S(1)}, u32[]{:S(2)}, u32[]{:S(2)}) %collective-permute-start.1) | collective-permute-done | bytes 40992 | tf_op jit(solution)/shard_map/ppermute | solution.py:469
  11.2 0.4 %spectra.1 = (f32[4,16,128]{2,1,0:T(8,128)S(1)}, f32[4,16,128]{2,1,0:T(8,128)S(1)}, f32[4,16,128]{2,1,0:T(8,128)S(1)}) custom-call(s32[1,8,128]{2,1,0:T(8,128)S(1)} %get-tuple-element.19.live_ref, bf16[5,4,256,128]{3,2,1,0:T(8,128)(2,1)S(1)} %green.1.green_ref, s16[5,2,16,128]{3,2,1,0:T(8,128)(2,1)S(1)} %collective-permute-done.refs_0_, ...), custom_call_target="tpu_custom_call" | custom-call | flops 3000000000 | bytes 12000000 | tf_op jit(solution)/shard_map/spectra/pallas_call | solution.py:333
  11.6 0.0 copy-start
  11.6 0.0 copy-start.1
  11.6 3.4 %collective-permute-start.3 = (f32[4,16,128]{2,1,0:T(8,128)S(1)}, f32[4,16,128]{2,1,0:T(8,128)S(1)}, u32[]{:S(2)}, u32[]{:S(2)}) collective-permute-start(f32[4,16,128]{2,1,0:T(8,128)S(1)} %get-tuple-element.26), channel_id=1, source_target_pairs={{0,12},{4,8},{8,4},{12,0},{1,13},{5,9},{9,5},{13,1},{2,14},{6,10},... | collective-permute-start | bytes 98312 | tf_op jit(solution)/shard_map/ppermute | solution.py:469
  15.1 1.1 %collective-permute-start.4 = (f32[4,16,128]{2,1,0:T(8,128)S(1)}, f32[4,16,128]{2,1,0:T(8,128)S(1)}, u32[]{:S(2)}, u32[]{:S(2)}) collective-permute-start(f32[4,16,128]{2,1,0:T(8,128)S(1)} %get-tuple-element.27), channel_id=1, source_target_pairs={{0,8},{4,12},{8,0},{12,4},{1,9},{5,13},{9,1},{13,5},{2,10},{6,14},... | collective-permute-start | bytes 98312 | tf_op jit(solution)/shard_map/ppermute | solution.py:469
  16.2 1.1 %own.1.refs_3_ = f32[4,16,128]{2,1,0:T(8,128)S(1)} custom-call(s32[1,8,128]{2,1,0:T(8,128)S(1)} %get-tuple-element.19.live_ref, bf16[5,4,256,128]{3,2,1,0:T(8,128)(2,1)S(1)} %green.1.green_ref, s16[5,2,16,128]{3,2,1,0:T(8,128)(2,1)S(1)} %get-tuple-element.29.refs_0_), custom_call_target="tpu_custom_call" | custom-call | flops 1000000000 | bytes 4000000 | tf_op jit(solution)/shard_map/own/pallas_call | solution.py:333
  17.4 0.7 %band.1 = (f32[32,512]{1,0:T(8,128)S(1)}, f32[8,512]{1,0:T(8,128)S(1)}) custom-call(s32[4]{0:T(128)S(1)} %copy-done.5, s32[4]{0:T(128)S(1)} %copy-done.6, f32[1,16,2,256]{3,2,1,0:T(2,128)S(1)} %copy-done.4, bf16[256,512]{1,0:T(8,128)(2,1)S(1)} %copy-done.2, bf16[256,512]{1,0:T(8,128)(2,1)S(1)} %copy-done.3), custom_call_target="tpu_custom_call" | custom-call | flops 25165824 | bytes 1000000 | tf_op jit(solution)/shard_map/band/pallas_call | solution.py:500
  18.1 1.9 %collective-permute-done.4.refs_1_ = f32[4,16,128]{2,1,0:T(8,128)S(1)} collective-permute-done((f32[4,16,128]{2,1,0:T(8,128)S(1)}, f32[4,16,128]{2,1,0:T(8,128)S(1)}, u32[]{:S(2)}, u32[]{:S(2)}) %collective-permute-start.4) | collective-permute-done | bytes 32800 | tf_op jit(solution)/shard_map/ppermute | solution.py:469
  20.0 0.3 %collective-permute-done.5.refs_2_ = f32[4,16,128]{2,1,0:T(8,128)S(1)} collective-permute-done((f32[4,16,128]{2,1,0:T(8,128)S(1)}, f32[4,16,128]{2,1,0:T(8,128)S(1)}, u32[]{:S(2)}, u32[]{:S(2)}) %collective-permute-start.5) | collective-permute-done | bytes 32800 | tf_op jit(solution)/shard_map/ppermute | solution.py:469
  20.3 0.1 excess.1.own_ref
  20.4 0.1 collective-permute-start.6
  20.5 1.2 %collective-permute-done.6.other_ref = f32[32,512]{1,0:T(8,128)S(1)} collective-permute-done((f32[32,512]{1,0:T(8,128)S(1)}, f32[32,512]{1,0:T(8,128)S(1)}, u32[]{:S(2)}, u32[]{:S(2)}) %collective-permute-start.6) | collective-permute-done | bytes 65568 | tf_op jit(solution)/shard_map/ppermute | solution.py:521
  21.8 0.8 %merge.1 = f32[1,16,2,256]{3,2,1,0:T(2,128)} custom-call(f32[32,512]{1,0:T(8,128)S(1)} %excess.1.own_ref, f32[32,512]{1,0:T(8,128)S(1)} %collective-permute-done.6.other_ref, f32[8,512]{1,0:T(8,128)S(1)} %get-tuple-element.30.weight_ref, f32[1,16,2,256]{3,2,1,0:T(2,128)S(1)} %copy-done.4, bf16[512,256]{1,0:T(8,128)(2,1)S(1)} %copy-done, ...), custom_call_target="tpu_custom_call" | custom-call | tf_op jit(solution)/shard_map/merge/pallas_call | solution.py:523
  (11 shorter events, 0.0 us)
Async XLA Ops:
  1.5 8.0 %collective-permute-start = (s16[5,2,16,128]{3,2,1,0:T(8,128)(2,1)S(1)}, s16[5,2,16,128]{3,2,1,0:T(8,128)(2,1)S(1)}, u32[]{:S(2)}, u32[]{:S(2)}) collective-permute-start(s16[5,2,16,128]{3,2,1,0:T(8,128)(2,1)S(1)} %get-tuple-element.23), channel_id=1, source_target_pairs={{0,8},{4,12},{8,0},{12,4},{1,9},{5,13},{9,1},{13,5},{2,10},{6,14},... | collective-permute-start | bytes 122888 | tf_op jit(solution)/shard_map/ppermute | solution.py:469
  5.4 5.8 %collective-permute-start.1 = (s16[5,2,16,128]{3,2,1,0:T(8,128)(2,1)S(1)}, s16[5,2,16,128]{3,2,1,0:T(8,128)(2,1)S(1)}, u32[]{:S(2)}, u32[]{:S(2)}) collective-permute-start(s16[5,2,16,128]{3,2,1,0:T(8,128)(2,1)S(1)} %get-tuple-element.24), channel_id=1, source_target_pairs={{0,12},{4,8},{8,4},{12,0},{1,13},{5,9},{9,5},{13,1},{2,14},{6,10},... | collective-permute-start | bytes 122888 | tf_op jit(solution)/shard_map/ppermute | solution.py:469
  6.8 4.5 %collective-permute-start.2 = (s16[5,2,16,128]{3,2,1,0:T(8,128)(2,1)S(1)}, s16[5,2,16,128]{3,2,1,0:T(8,128)(2,1)S(1)}, u32[]{:S(2)}, u32[]{:S(2)}) collective-permute-start(s16[5,2,16,128]{3,2,1,0:T(8,128)(2,1)S(1)} %get-tuple-element.25), channel_id=1, source_target_pairs={{0,4},{4,0},{8,12},{12,8},{1,5},{5,1},{9,13},{13,9},{2,6},{6,2},{1... | collective-permute-start | bytes 122888 | tf_op jit(solution)/shard_map/ppermute | solution.py:469
  9.4 7.9 %copy-start.2 = (bf16[256,512]{1,0:T(8,128)(2,1)S(1)}, bf16[256,512]{1,0:T(8,128)(2,1)}, u32[]{:S(2)}) copy-start(bf16[256,512]{1,0:T(8,128)(2,1)} %constant.8.clone.table_high) | copy-start | bytes 786436
  9.4 7.9 %copy-start.3 = (bf16[256,512]{1,0:T(8,128)(2,1)S(1)}, bf16[256,512]{1,0:T(8,128)(2,1)}, u32[]{:S(2)}) copy-start(bf16[256,512]{1,0:T(8,128)(2,1)} %constant.9.clone.table_low) | copy-start | bytes 786436
  9.5 7.9 %copy-start.4 = (f32[1,16,2,256]{3,2,1,0:T(2,128)S(1)}, f32[1,16,2,256]{3,2,1,0:T(2,128)}, u32[]{:S(2)}) copy-start(f32[1,16,2,256]{3,2,1,0:T(2,128)} %high_ref.3) | copy-start | bytes 98308
  9.5 7.9 %copy-start.5 = (s32[4]{0:T(128)S(1)}, s32[4]{0:T(128)}, u32[]{:S(2)}) copy-start(s32[4]{0:T(128)} %refs_0_.1) | copy-start | bytes 52
  9.5 7.9 %copy-start.6 = (s32[4]{0:T(128)S(1)}, s32[4]{0:T(128)}, u32[]{:S(2)}) copy-start(s32[4]{0:T(128)} %crossover_ref.1) | copy-start | bytes 52
  11.6 10.2 %copy-start = (bf16[512,256]{1,0:T(8,128)(2,1)S(1)}, bf16[512,256]{1,0:T(8,128)(2,1)}, u32[]{:S(2)}) copy-start(bf16[512,256]{1,0:T(8,128)(2,1)} %constant.10.clone.table_high) | copy-start | bytes 786436
  11.6 10.1 %copy-start.1 = (bf16[512,256]{1,0:T(8,128)(2,1)S(1)}, bf16[512,256]{1,0:T(8,128)(2,1)}, u32[]{:S(2)}) copy-start(bf16[512,256]{1,0:T(8,128)(2,1)} %constant.11.clone.table_low) | copy-start | bytes 786436
  11.6 6.5 %collective-permute-start.3 = (f32[4,16,128]{2,1,0:T(8,128)S(1)}, f32[4,16,128]{2,1,0:T(8,128)S(1)}, u32[]{:S(2)}, u32[]{:S(2)}) collective-permute-start(f32[4,16,128]{2,1,0:T(8,128)S(1)} %get-tuple-element.26), channel_id=1, source_target_pairs={{0,12},{4,8},{8,4},{12,0},{1,13},{5,9},{9,5},{13,1},{2,14},{6,10},... | collective-permute-start | bytes 98312 | tf_op jit(solution)/shard_map/ppermute | solution.py:469
  15.1 5.0 %collective-permute-start.4 = (f32[4,16,128]{2,1,0:T(8,128)S(1)}, f32[4,16,128]{2,1,0:T(8,128)S(1)}, u32[]{:S(2)}, u32[]{:S(2)}) collective-permute-start(f32[4,16,128]{2,1,0:T(8,128)S(1)} %get-tuple-element.27), channel_id=1, source_target_pairs={{0,8},{4,12},{8,0},{12,4},{1,9},{5,13},{9,1},{13,5},{2,10},{6,14},... | collective-permute-start | bytes 98312 | tf_op jit(solution)/shard_map/ppermute | solution.py:469
  16.1 4.2 %collective-permute-start.5 = (f32[4,16,128]{2,1,0:T(8,128)S(1)}, f32[4,16,128]{2,1,0:T(8,128)S(1)}, u32[]{:S(2)}, u32[]{:S(2)}) collective-permute-start(f32[4,16,128]{2,1,0:T(8,128)S(1)} %get-tuple-element.28), channel_id=1, source_target_pairs={{0,4},{4,0},{8,12},{12,8},{1,5},{5,1},{9,13},{13,9},{2,6},{6,2},{1... | collective-permute-start | bytes 98312 | tf_op jit(solution)/shard_map/ppermute | solution.py:469
  20.4 1.3 %collective-permute-start.6 = (f32[32,512]{1,0:T(8,128)S(1)}, f32[32,512]{1,0:T(8,128)S(1)}, u32[]{:S(2)}, u32[]{:S(2)}) collective-permute-start(f32[32,512]{1,0:T(8,128)S(1)} %excess.1.own_ref), channel_id=1, source_target_pairs={{0,1},{1,0},{2,3},{3,2},{4,5},{5,4},{6,7},{7,6},{8,9},{9,8},{10,11... | collective-permute-start | bytes 196616 | tf_op jit(solution)/shard_map/ppermute | solution.py:521

commit v2 on v1

--- a/solution.py
+++ b/solution.py
@@ -64,9 +64,9 @@
 
 
 def pack_kernel(blocks_here, block_points, onset_scale, slip_scale, *refs):
-    sources, later_sources, strain_hbm, outs = refs[:5], refs[5:7], refs[7], refs[8:-12]
-    live_ref, head_ref, later_targets = refs[-12], refs[-11], refs[-10:-8]
-    targets, sems, later_sems, head_sem = refs[-8:-3], refs[-3], refs[-2], refs[-1]
+    sources, later_sources, strain_hbm, outs = refs[:5], refs[5:7], refs[7], refs[8:-13]
+    live_ref, head_ref, later_targets = refs[-13], refs[-12], refs[-11:-9]
+    targets, coded, sems, later_sems, head_sem = refs[-9:-4], *refs[-4:]
     row_ref, blocks_ref, count_ref, slip_ref, onset_ref = targets
     copies = fetch(sources, targets, sems)
     later = fetch(later_sources, later_targets, later_sems)
@@ -105,16 +105,14 @@
         onset = jnp.clip(onset.astype(jnp.int32) - 32768, -32768, 32767).astype(jnp.int16)
         slip = slip_ref[0, :, pl.ds(offset, block_points)].astype(f32) * slip_scale
         slip = slip.astype(jnp.int32).astype(jnp.int16)
-        for step, out in enumerate(outs):
-
-            @pl.when(owner == jnp.bitwise_xor(me, step))
-            def _():
-                out[local, 0] = onset
-                out[local, 1] = slip
-
+        place = jnp.bitwise_xor(me, owner) * blocks_here + local
+        coded[place, 0] = onset
+        coded[place, 1] = slip
         return carry
 
     lax.fori_loop(0, count_ref[rupture], visit, 0)
+    for step, out in enumerate(outs):
+        out[...] = coded[step * blocks_here : (step + 1) * blocks_here]
     for copy in later:
         copy.wait()
 
@@ -279,49 +277,50 @@
         low = max(first_step, word * steps_per_word)
         high = min(first_step + steps, (word + 1) * steps_per_word)
 
-        def visit(place, carry):
-            flag = jnp.right_shift(flags, place - word * steps_per_word * blocks_here) & 1
-
-            @pl.when(flag == 1)
-            def _():
-                step = place // blocks_here
-                local = place - step * blocks_here
-                source = place - first_step * blocks_here
-                onset = held[source, 0].astype(jnp.int32).astype(f32) + 32768.0
-                slip = held[source, 1].astype(jnp.int32).astype(f32) * (1.0 / slip_scale)
-                cycles = onset * (1.0 / (onset_scale * samples))
-                one = circle(cycles)
-                two = turn(one, one)
-                four = turn(two, two)
-                start = circle(cycles * first_bin)
-                now = [(slip * start[0], slip * start[1])]
-                now.append(turn(now[0], one))
-                now.append(turn(now[0], two))
-                now.append(turn(now[1], two))
-                after = [turn(wave, four) for wave in now]
-                double = 2.0 * four[0]
-                for j in range(bins // 4):
-                    rows = pl.ds(j * variations, variations)
-                    for r in range(4):
-                        waves[r, rows, 0:block_points] = now[r][0].astype(bf16)
-                        waves[r, rows, block_points : 2 * block_points] = now[r][1].astype(bf16)
-                    later = [
-                        (double * after[r][0] - now[r][0], double * after[r][1] - now[r][1])
-                        for r in range(4)
-                    ]
-                    now, after = after, later
+        def visit(left):
+            bit = 31 - lax.clz(left)
+            place = bit + word * steps_per_word * blocks_here
+            step = place // blocks_here
+            local = place - step * blocks_here
+            source = place - first_step * blocks_here
+            onset = held[source, 0].astype(jnp.int32).astype(f32) + 32768.0
+            slip = held[source, 1].astype(jnp.int32).astype(f32) * (1.0 / slip_scale)
+            cycles = onset * (1.0 / (onset_scale * samples))
+            one = circle(cycles)
+            two = turn(one, one)
+            four = turn(two, two)
+            start = circle(cycles * first_bin)
+            now = [(slip * start[0], slip * start[1])]
+            now.append(turn(now[0], one))
+            now.append(turn(now[0], two))
+            now.append(turn(now[1], two))
+            after = [turn(wave, four) for wave in now]
+            double = 2.0 * four[0]
+            for j in range(bins // 4):
+                rows = pl.ds(j * variations, variations)
                 for r in range(4):
-                    product = jnp.dot(waves[r], green_ref[local, r], preferred_element_type=f32)
-                    found = product[0:variations]
-                    for j in range(1, bins // 4):
-                        found = jnp.where(
-                            quarter == j, product[j * variations : (j + 1) * variations], found
-                        )
-                    total[step - first_step, r] += found
-
-            return carry
-
-        lax.fori_loop(low * blocks_here, high * blocks_here, visit, 0)
+                    waves[r, rows, 0:block_points] = now[r][0].astype(bf16)
+                    waves[r, rows, block_points : 2 * block_points] = now[r][1].astype(bf16)
+                later = [
+                    (double * after[r][0] - now[r][0], double * after[r][1] - now[r][1])
+                    for r in range(4)
+                ]
+                now, after = after, later
+            for r in range(4):
+                product = jnp.dot(waves[r], green_ref[local, r], preferred_element_type=f32)
+                found = product[0:variations]
+                for j in range(1, bins // 4):
+                    found = jnp.where(
+                        quarter == j, product[j * variations : (j + 1) * variations], found
+                    )
+                total[step - first_step, r] += found
+
+            return left ^ jnp.left_shift(1, bit)
+
+        first = (low - word * steps_per_word) * blocks_here
+        last = (high - word * steps_per_word) * blocks_here
+        flags = flags & ((1 << last) - (1 << first))
+        lax.while_loop(lambda left: left != 0, visit, flags)
     for step in range(steps):
         outs[step][...] = total[step]
 
@@ -446,6 +445,7 @@
         scratch_shapes=scalar_scratch((rupture_row, rupture_blocks, block_count))
         + [pltpu.VMEM(a.shape, a.dtype) for a in (slip_amplitude, onset_time)]
         + [
+            pltpu.VMEM((pt_size * blocks_here,) + pack_shape.shape[1:], jnp.int16),
             pltpu.SemaphoreType.DMA((5,)),
             pltpu.SemaphoreType.DMA((2,)),
             pltpu.SemaphoreType.DMA,

time: 22.5 us -> 22 us (0.978)
  waiting for transfers between devices: 5.22 us -> 2.97 us
  Pallas kernels: 7.1 us -> 8.52 us
    ppermute x6, waiting for transfers between devices: 3.98 us -> 1.73 us  [swap(): return lax.ppermute(value, 'pt', [(i, i ^ step) for i in range(pt_size)])]
    pallas_call x2, Pallas kernels: 1.52 us -> 2.69 us  [spectra_call(): pl.pallas_call(functools.partial(spectra_kernel, blocks_here, 4 * bins_he...]
    pallas_call x1, Pallas kernels: 2.41 us -> 2.85 us  [body(): pl.pallas_call(functools.partial(green_kernel, pt_size), out_shape=jax.Sh...]
where the time goes in v2:
time: 22 us; the launch traced here: 21.9 us
  starting transfers between devices  10.2 us (46%)
  Pallas kernels  8.52 us (39%)
  waiting for transfers between devices  2.97 us (14%)
    ppermute x6, starting transfers between devices, swap(): return lax.ppermute(value, 'pt', [(i, i ^ step) for i in range(pt_size)])  10.1 us
    pallas_call x1, Pallas kernels, body(): pl.pallas_call(functools.partial(green_kernel, pt_size), out_shape=jax.Sh...  2.85 us
    pallas_call x2, Pallas kernels, spectra_call(): pl.pallas_call(functools.partial(spectra_kernel, blocks_here, 4 * bins_he...  2.69 us
    ppermute x6, waiting for transfers between devices, swap(): return lax.ppermute(value, 'pt', [(i, i ^ step) for i in range(pt_size)])  1.73 us
    pallas_call x1, Pallas kernels, body(): pl.pallas_call(functools.partial(pack_kernel, blocks_here, block_points,...  1.32 us
    ppermute x1, waiting for transfers between devices, body(): other = lax.ppermute(excess, 'cmp', [(0, 1), (1, 0)])  1.24 us
    pallas_call x1, Pallas kernels, body(): pl.pallas_call(merge_kernel, out_shape=jax.ShapeDtypeStruct(high_band.sha...  0.83 us
    pallas_call x1, Pallas kernels, body(): pl.pallas_call(functools.partial(band_kernel, bins, samples), out_shape=[...  0.74 us
  transfers between devices with their start and end apart: 7, of which 4 were waited for; matrix products, arithmetic and copies ran while one was open for 0% of the time, Pallas kernels for 19%

profile of v2, /device:TPU:0, one launch (start us, length us, event | category | flops | bytes accessed | tf_op | source)
XLA Modules:
  0.0 21.9 jit_solution(15790862054504686472)
XLA Ops:
  0.0 1.3 %pack.1 = (s16[5,2,16,128]{3,2,1,0:T(8,128)(2,1)S(1)}, s16[5,2,16,128]{3,2,1,0:T(8,128)(2,1)S(1)}, s16[5,2,16,128]{3,2,1,0:T(8,128)(2,1)S(1)}, s16[5,2,16,128]{3...) custom-call(s32[4]{0:T(128)} %refs_0_.1, ...), custom_call_target="tpu_custom_call" | custom-call | tf_op jit(solution)/shard_map/pack/pallas_call | solution.py:438
  1.3 4.1 %collective-permute-start = (s16[5,2,16,128]{3,2,1,0:T(8,128)(2,1)S(1)}, s16[5,2,16,128]{3,2,1,0:T(8,128)(2,1)S(1)}, u32[]{:S(2)}, u32[]{:S(2)}) collective-permute-start(s16[5,2,16,128]{3,2,1,0:T(8,128)(2,1)S(1)} %get-tuple-element.23), channel_id=1, source_target_pairs={{0,8},{4,12},{8,0},{12,4},{1,9},{5,13},{9,1},{13,5},{2,10},{6,14},... | collective-permute-start | bytes 122888 | tf_op jit(solution)/shard_map/ppermute | solution.py:469
  5.4 1.3 %collective-permute-start.1 = (s16[5,2,16,128]{3,2,1,0:T(8,128)(2,1)S(1)}, s16[5,2,16,128]{3,2,1,0:T(8,128)(2,1)S(1)}, u32[]{:S(2)}, u32[]{:S(2)}) collective-permute-start(s16[5,2,16,128]{3,2,1,0:T(8,128)(2,1)S(1)} %get-tuple-element.24), channel_id=1, source_target_pairs={{0,12},{4,8},{8,4},{12,0},{1,13},{5,9},{9,5},{13,1},{2,14},{6,10},... | collective-permute-start | bytes 122888 | tf_op jit(solution)/shard_map/ppermute | solution.py:469
  6.8 0.2 %collective-permute-start.2 = (s16[5,2,16,128]{3,2,1,0:T(8,128)(2,1)S(1)}, s16[5,2,16,128]{3,2,1,0:T(8,128)(2,1)S(1)}, u32[]{:S(2)}, u32[]{:S(2)}) collective-permute-start(s16[5,2,16,128]{3,2,1,0:T(8,128)(2,1)S(1)} %get-tuple-element.25), channel_id=1, source_target_pairs={{0,4},{4,0},{8,12},{12,8},{1,5},{5,1},{9,13},{13,9},{2,6},{6,2},{1... | collective-permute-start | bytes 122888 | tf_op jit(solution)/shard_map/ppermute | solution.py:469
  7.0 2.9 %green.1.green_ref = bf16[5,4,256,128]{3,2,1,0:T(8,128)(2,1)S(1)} custom-call(s32[1,8,128]{2,1,0:T(8,128)S(1)} %get-tuple-element.19.live_ref, bf16[3072,128]{1,0:T(8,128)(2,1)S(1)} %get-tuple-element.20.head_ref, bf16[15360,128]{1,0:T(8,128)(2,1)} %bitcast.2, f32[5,24]{1,0:T(8,128)S(1)} %get-tuple-element.21.scale_ref, ...), custom_call_target="tpu_custom_call" | custom-call | flops 3932160 | bytes 6000000 | tf_op jit(solution)/shard_map/green/pallas_call | solution.py:477
  9.9 0.0 copy-start.2
  9.9 0.0 copy-start.3
  9.9 0.0 copy-start.4
  9.9 0.0 copy-start.6
  9.9 1.3 %collective-permute-done.1.refs_1_ = s16[5,2,16,128]{3,2,1,0:T(8,128)(2,1)S(1)} collective-permute-done((s16[5,2,16,128]{3,2,1,0:T(8,128)(2,1)S(1)}, s16[5,2,16,128]{3,2,1,0:T(8,128)(2,1)S(1)}, u32[]{:S(2)}, u32[]{:S(2)}) %collective-permute-start.1) | collective-permute-done | bytes 40992 | tf_op jit(solution)/shard_map/ppermute | solution.py:469
  11.2 2.0 %spectra.1 = (f32[4,16,128]{2,1,0:T(8,128)S(1)}, f32[4,16,128]{2,1,0:T(8,128)S(1)}, f32[4,16,128]{2,1,0:T(8,128)S(1)}) custom-call(s32[1,8,128]{2,1,0:T(8,128)S(1)} %get-tuple-element.19.live_ref, bf16[5,4,256,128]{3,2,1,0:T(8,128)(2,1)S(1)} %green.1.green_ref, s16[5,2,16,128]{3,2,1,0:T(8,128)(2,1)S(1)} %collective-permute-done.refs_0_, ...), custom_call_target="tpu_custom_call" | custom-call | flops 3000000000 | bytes 12000000 | tf_op jit(solution)/shard_map/spectra/pallas_call | solution.py:332
  13.3 0.0 copy-start
  13.3 0.0 copy-start.1
  13.3 0.7 %collective-permute-start.3 = (f32[4,16,128]{2,1,0:T(8,128)S(1)}, f32[4,16,128]{2,1,0:T(8,128)S(1)}, u32[]{:S(2)}, u32[]{:S(2)}) collective-permute-start(f32[4,16,128]{2,1,0:T(8,128)S(1)} %get-tuple-element.26), channel_id=1, source_target_pairs={{0,12},{4,8},{8,4},{12,0},{1,13},{5,9},{9,5},{13,1},{2,14},{6,10},... | collective-permute-start | bytes 98312 | tf_op jit(solution)/shard_map/ppermute | solution.py:469
  14.0 0.3 %collective-permute-start.4 = (f32[4,16,128]{2,1,0:T(8,128)S(1)}, f32[4,16,128]{2,1,0:T(8,128)S(1)}, u32[]{:S(2)}, u32[]{:S(2)}) collective-permute-start(f32[4,16,128]{2,1,0:T(8,128)S(1)} %get-tuple-element.27), channel_id=1, source_target_pairs={{0,8},{4,12},{8,0},{12,4},{1,9},{5,13},{9,1},{13,5},{2,10},{6,14},... | collective-permute-start | bytes 98312 | tf_op jit(solution)/shard_map/ppermute | solution.py:469
  14.4 3.4 %collective-permute-start.5 = (f32[4,16,128]{2,1,0:T(8,128)S(1)}, f32[4,16,128]{2,1,0:T(8,128)S(1)}, u32[]{:S(2)}, u32[]{:S(2)}) collective-permute-start(f32[4,16,128]{2,1,0:T(8,128)S(1)} %get-tuple-element.28), channel_id=1, source_target_pairs={{0,4},{4,0},{8,12},{12,8},{1,5},{5,1},{9,13},{13,9},{2,6},{6,2},{1... | collective-permute-start | bytes 98312 | tf_op jit(solution)/shard_map/ppermute | solution.py:469
  17.8 0.7 %own.1.refs_3_ = f32[4,16,128]{2,1,0:T(8,128)S(1)} custom-call(s32[1,8,128]{2,1,0:T(8,128)S(1)} %get-tuple-element.19.live_ref, bf16[5,4,256,128]{3,2,1,0:T(8,128)(2,1)S(1)} %green.1.green_ref, s16[5,2,16,128]{3,2,1,0:T(8,128)(2,1)S(1)} %get-tuple-element.29.refs_0_), custom_call_target="tpu_custom_call" | custom-call | flops 1000000000 | bytes 4000000 | tf_op jit(solution)/shard_map/own/pallas_call | solution.py:332
  18.5 0.7 %band.1 = (f32[32,512]{1,0:T(8,128)S(1)}, f32[8,512]{1,0:T(8,128)S(1)}) custom-call(s32[4]{0:T(128)S(1)} %copy-done.5, s32[4]{0:T(128)S(1)} %copy-done.6, f32[1,16,2,256]{3,2,1,0:T(2,128)S(1)} %copy-done.4, bf16[256,512]{1,0:T(8,128)(2,1)S(1)} %copy-done.2, bf16[256,512]{1,0:T(8,128)(2,1)S(1)} %copy-done.3), custom_call_target="tpu_custom_call" | custom-call | flops 25165824 | bytes 1000000 | tf_op jit(solution)/shard_map/band/pallas_call | solution.py:500
  19.2 0.3 %collective-permute-done.4.refs_1_ = f32[4,16,128]{2,1,0:T(8,128)S(1)} collective-permute-done((f32[4,16,128]{2,1,0:T(8,128)S(1)}, f32[4,16,128]{2,1,0:T(8,128)S(1)}, u32[]{:S(2)}, u32[]{:S(2)}) %collective-permute-start.4) | collective-permute-done | bytes 32800 | tf_op jit(solution)/shard_map/ppermute | solution.py:469
  19.5 0.1 collective-permute-done.5.refs_2_
  19.6 0.1 excess.1.own_ref
  19.7 0.1 collective-permute-start.6
  19.8 1.2 %collective-permute-done.6.other_ref = f32[32,512]{1,0:T(8,128)S(1)} collective-permute-done((f32[32,512]{1,0:T(8,128)S(1)}, f32[32,512]{1,0:T(8,128)S(1)}, u32[]{:S(2)}, u32[]{:S(2)}) %collective-permute-start.6) | collective-permute-done | bytes 65568 | tf_op jit(solution)/shard_map/ppermute | solution.py:521
  21.1 0.8 %merge.1 = f32[1,16,2,256]{3,2,1,0:T(2,128)} custom-call(f32[32,512]{1,0:T(8,128)S(1)} %excess.1.own_ref, f32[32,512]{1,0:T(8,128)S(1)} %collective-permute-done.6.other_ref, f32[8,512]{1,0:T(8,128)S(1)} %get-tuple-element.30.weight_ref, f32[1,16,2,256]{3,2,1,0:T(2,128)S(1)} %copy-done.4, bf16[512,256]{1,0:T(8,128)(2,1)S(1)} %copy-done, ...), custom_call_target="tpu_custom_call" | custom-call | tf_op jit(solution)/shard_map/merge/pallas_call | solution.py:523
  (11 shorter events, 0.0 us)
Async XLA Ops:
  1.3 8.6 %collective-permute-start = (s16[5,2,16,128]{3,2,1,0:T(8,128)(2,1)S(1)}, s16[5,2,16,128]{3,2,1,0:T(8,128)(2,1)S(1)}, u32[]{:S(2)}, u32[]{:S(2)}) collective-permute-start(s16[5,2,16,128]{3,2,1,0:T(8,128)(2,1)S(1)} %get-tuple-element.23), channel_id=1, source_target_pairs={{0,8},{4,12},{8,0},{12,4},{1,9},{5,13},{9,1},{13,5},{2,10},{6,14},... | collective-permute-start | bytes 122888 | tf_op jit(solution)/shard_map/ppermute | solution.py:469
  5.4 5.8 %collective-permute-start.1 = (s16[5,2,16,128]{3,2,1,0:T(8,128)(2,1)S(1)}, s16[5,2,16,128]{3,2,1,0:T(8,128)(2,1)S(1)}, u32[]{:S(2)}, u32[]{:S(2)}) collective-permute-start(s16[5,2,16,128]{3,2,1,0:T(8,128)(2,1)S(1)} %get-tuple-element.24), channel_id=1, source_target_pairs={{0,12},{4,8},{8,4},{12,0},{1,13},{5,9},{9,5},{13,1},{2,14},{6,10},... | collective-permute-start | bytes 122888 | tf_op jit(solution)/shard_map/ppermute | solution.py:469
  6.8 4.5 %collective-permute-start.2 = (s16[5,2,16,128]{3,2,1,0:T(8,128)(2,1)S(1)}, s16[5,2,16,128]{3,2,1,0:T(8,128)(2,1)S(1)}, u32[]{:S(2)}, u32[]{:S(2)}) collective-permute-start(s16[5,2,16,128]{3,2,1,0:T(8,128)(2,1)S(1)} %get-tuple-element.25), channel_id=1, source_target_pairs={{0,4},{4,0},{8,12},{12,8},{1,5},{5,1},{9,13},{13,9},{2,6},{6,2},{1... | collective-permute-start | bytes 122888 | tf_op jit(solution)/shard_map/ppermute | solution.py:469
  9.9 8.5 %copy-start.2 = (bf16[256,512]{1,0:T(8,128)(2,1)S(1)}, bf16[256,512]{1,0:T(8,128)(2,1)}, u32[]{:S(2)}) copy-start(bf16[256,512]{1,0:T(8,128)(2,1)} %constant.8.clone.table_high) | copy-start | bytes 786436
  9.9 8.5 %copy-start.3 = (bf16[256,512]{1,0:T(8,128)(2,1)S(1)}, bf16[256,512]{1,0:T(8,128)(2,1)}, u32[]{:S(2)}) copy-start(bf16[256,512]{1,0:T(8,128)(2,1)} %constant.9.clone.table_low) | copy-start | bytes 786436
  9.9 8.5 %copy-start.4 = (f32[1,16,2,256]{3,2,1,0:T(2,128)S(1)}, f32[1,16,2,256]{3,2,1,0:T(2,128)}, u32[]{:S(2)}) copy-start(f32[1,16,2,256]{3,2,1,0:T(2,128)} %high_ref.3) | copy-start | bytes 98308
  9.9 8.5 %copy-start.5 = (s32[4]{0:T(128)S(1)}, s32[4]{0:T(128)}, u32[]{:S(2)}) copy-start(s32[4]{0:T(128)} %refs_0_.1) | copy-start | bytes 52
  9.9 8.5 %copy-start.6 = (s32[4]{0:T(128)S(1)}, s32[4]{0:T(128)}, u32[]{:S(2)}) copy-start(s32[4]{0:T(128)} %crossover_ref.1) | copy-start | bytes 52
  13.3 7.8 %copy-start = (bf16[512,256]{1,0:T(8,128)(2,1)S(1)}, bf16[512,256]{1,0:T(8,128)(2,1)}, u32[]{:S(2)}) copy-start(bf16[512,256]{1,0:T(8,128)(2,1)} %constant.10.clone.table_high) | copy-start | bytes 786436
  13.3 7.8 %copy-start.1 = (bf16[512,256]{1,0:T(8,128)(2,1)S(1)}, bf16[512,256]{1,0:T(8,128)(2,1)}, u32[]{:S(2)}) copy-start(bf16[512,256]{1,0:T(8,128)(2,1)} %constant.11.clone.table_low) | copy-start | bytes 786436
  13.3 5.9 %collective-permute-start.3 = (f32[4,16,128]{2,1,0:T(8,128)S(1)}, f32[4,16,128]{2,1,0:T(8,128)S(1)}, u32[]{:S(2)}, u32[]{:S(2)}) collective-permute-start(f32[4,16,128]{2,1,0:T(8,128)S(1)} %get-tuple-element.26), channel_id=1, source_target_pairs={{0,12},{4,8},{8,4},{12,0},{1,13},{5,9},{9,5},{13,1},{2,14},{6,10},... | collective-permute-start | bytes 98312 | tf_op jit(solution)/shard_map/ppermute | solution.py:469
  14.0 5.5 %collective-permute-start.4 = (f32[4,16,128]{2,1,0:T(8,128)S(1)}, f32[4,16,128]{2,1,0:T(8,128)S(1)}, u32[]{:S(2)}, u32[]{:S(2)}) collective-permute-start(f32[4,16,128]{2,1,0:T(8,128)S(1)} %get-tuple-element.27), channel_id=1, source_target_pairs={{0,8},{4,12},{8,0},{12,4},{1,9},{5,13},{9,1},{13,5},{2,10},{6,14},... | collective-permute-start | bytes 98312 | tf_op jit(solution)/shard_map/ppermute | solution.py:469
  14.4 5.3 %collective-permute-start.5 = (f32[4,16,128]{2,1,0:T(8,128)S(1)}, f32[4,16,128]{2,1,0:T(8,128)S(1)}, u32[]{:S(2)}, u32[]{:S(2)}) collective-permute-start(f32[4,16,128]{2,1,0:T(8,128)S(1)} %get-tuple-element.28), channel_id=1, source_target_pairs={{0,4},{4,0},{8,12},{12,8},{1,5},{5,1},{9,13},{13,9},{2,6},{6,2},{1... | collective-permute-start | bytes 98312 | tf_op jit(solution)/shard_map/ppermute | solution.py:469
  19.7 1.3 %collective-permute-start.6 = (f32[32,512]{1,0:T(8,128)S(1)}, f32[32,512]{1,0:T(8,128)S(1)}, u32[]{:S(2)}, u32[]{:S(2)}) collective-permute-start(f32[32,512]{1,0:T(8,128)S(1)} %excess.1.own_ref), channel_id=1, source_target_pairs={{0,1},{1,0},{2,3},{3,2},{4,5},{5,4},{6,7},{7,6},{8,9},{9,8},{10,11... | collective-permute-start | bytes 196616 | tf_op jit(solution)/shard_map/ppermute | solution.py:521

commit v3 on v2

--- a/solution.py
+++ b/solution.py
@@ -64,15 +64,12 @@
 
 
 def pack_kernel(blocks_here, block_points, onset_scale, slip_scale, *refs):
-    sources, later_sources, strain_hbm, outs = refs[:5], refs[5:7], refs[7], refs[8:-13]
-    live_ref, head_ref, later_targets = refs[-13], refs[-12], refs[-11:-9]
-    targets, coded, sems, later_sems, head_sem = refs[-9:-4], *refs[-4:]
+    sources, later_sources, outs = refs[:5], refs[5:7], refs[8:-11]
+    live_ref, later_targets = refs[-11], refs[-10:-8]
+    targets, coded, sems, later_sems = refs[-8:-3], *refs[-3:]
     row_ref, blocks_ref, count_ref, slip_ref, onset_ref = targets
     copies = fetch(sources, targets, sems)
     later = fetch(later_sources, later_targets, later_sems)
-    head = pltpu.make_async_copy(strain_hbm.at[pl.ds(0, head_ref.shape[0])], head_ref, head_sem)
-    head.start()
-    later.append(head)
     for copy in copies[:3]:
         copy.wait()
     me = lax.axis_index("pt")
@@ -126,24 +123,15 @@
 
 
 def green_kernel(
-    steps, live_ref, head_ref, strain_hbm, scale_ref, mechanism_ref, out_ref, strain_ref, factor_ref, sems
+    steps, live_ref, strain_ref, scale_ref, mechanism_ref, out_ref, factor_ref
 ):
     rows, octet = 24, 8
     wide, depth = octet * rows, factor_ref.shape[1]
     blocks_here = scale_ref.shape[0]
-    bins = strain_ref.shape[2]
+    bins = strain_ref.shape[1]
     block_points = mechanism_ref.shape[1] // blocks_here
     per_block = block_points * rows
 
-    def strain_copy(b, source=strain_hbm):
-        place = pl.ds(pl.multiple_of(b * per_block, per_block), per_block)
-        target = strain_ref.at[b, pl.ds(0, per_block)]
-        return pltpu.make_async_copy(source.at[place], target, sems.at[b])
-
-    for b in range(blocks_here):
-        strain_copy(b, head_ref if b * per_block < head_ref.shape[0] else strain_hbm).start()
-    for b in range(blocks_here):
-        strain_ref[b, per_block:, :] = jnp.zeros((depth - wide, bins), bf16)
     column = lax.broadcasted_iota(jnp.int32, (18, depth), 1) % rows
     spread_six = column % 6 == lax.broadcasted_iota(jnp.int32, (18, depth), 0) % 6
     column = lax.broadcasted_iota(jnp.int32, (3 * rows, depth), 1) % rows
@@ -164,12 +152,18 @@
         factor_ref[place, :] = moments[place] * scales[b : b + 1]
     row = lax.broadcasted_iota(jnp.int32, (2 * octet, depth), 0)
     column = lax.broadcasted_iota(jnp.int32, (2 * octet, depth), 1)
-    same_point = column // rows == row % octet
-    part = (column % rows) // 6
-    masks = [
-        jnp.where(same_point & (part == 2 * h + row // octet), 1.0, 0.0).astype(bf16)
-        for h in range(2)
-    ]
+
+    def point_masks(first_column):
+        place = column - first_column
+        mine = (place // rows == row % octet) & (place >= 0)
+        part = (place % rows) // 6
+        return [
+            jnp.where(mine & (part == 2 * h + row // octet), 1.0, 0.0).astype(bf16)
+            for h in range(2)
+        ]
+
+    spare = depth - wide
+    usual, at_end = point_masks(0), point_masks(spare)
     lane = lax.broadcasted_iota(jnp.int32, (2 * octet, bins), 1) % 4
     even, low_lane = lane % 2 == 0, lane < 2
 
@@ -180,7 +174,6 @@
     live = [jnp.max(live_ref[word]) for word in range(words)]
 
     def one_block(b, carry):
-        strain_copy(b).wait()
         flags = 0
         for step in range(steps):
             place = step % steps_per_word * blocks_here + b
@@ -200,6 +193,10 @@
                     b * block_points + pair * 2 * octet + half * octet, octet
                 )
                 here = factor_ref[pl.ds(first, octet)]
+                last = (pair + 1) * 2 * octet == block_points and half == 1
+                masks = at_end if last else usual
+                if last:
+                    here = pltpu.roll(here, spare, 1)
                 here = jnp.concatenate([here, here], axis=0)
                 coarse = here.astype(bf16)
                 fine = (here - coarse.astype(f32)).astype(bf16)
@@ -207,8 +204,8 @@
                     [coarse * masks[0], coarse * masks[1], fine * masks[0], fine * masks[1]],
                     axis=0,
                 )
-                own = (pair * 2 + half) * wide
-                strain = strain_ref[b, own : own + depth, :]
+                begin = pl.multiple_of(first * rows - (spare if last else 0), 64)
+                strain = strain_ref[pl.ds(begin, depth), :]
                 both = jnp.dot(left, strain, preferred_element_type=f32)
                 for k in range(4):
                     spectra[k].append(
@@ -430,25 +427,22 @@
     assert samples == 2 * bins and strain_rows == 24
 
     strain_lines = strain_green.reshape(points_here * strain_rows, bins_here)
-    head_blocks = 1
-    head_shape = jax.ShapeDtypeStruct((head_blocks * block_points * strain_rows, bins_here), bf16)
     pack_shape = jax.ShapeDtypeStruct((blocks_here, 2, variations, block_points), jnp.int16)
     live_shape = jax.ShapeDtypeStruct((live_words(pt_size, blocks_here)[1], 8, 128), jnp.int32)
     onset_scale, slip_scale = 512.0, 1024.0
-    *packed, live, head, scale_here, mechanism_here = pl.pallas_call(
+    *packed, live, scale_here, mechanism_here = pl.pallas_call(
         functools.partial(pack_kernel, blocks_here, block_points, onset_scale, slip_scale),
         out_shape=[pack_shape] * pt_size
-        + [live_shape, head_shape]
+        + [live_shape]
         + [jax.ShapeDtypeStruct(a.shape, a.dtype) for a in (green_scale, mechanism)],
         in_specs=[HBM] * 8,
-        out_specs=[VMEM] * (pt_size + 4),
+        out_specs=[VMEM] * (pt_size + 3),
         scratch_shapes=scalar_scratch((rupture_row, rupture_blocks, block_count))
         + [pltpu.VMEM(a.shape, a.dtype) for a in (slip_amplitude, onset_time)]
         + [
             pltpu.VMEM((pt_size * blocks_here,) + pack_shape.shape[1:], jnp.int16),
             pltpu.SemaphoreType.DMA((5,)),
             pltpu.SemaphoreType.DMA((2,)),
-            pltpu.SemaphoreType.DMA,
         ],
         compiler_params=params(),
         name="pack",
@@ -477,17 +471,20 @@
     green = pl.pallas_call(
         functools.partial(green_kernel, pt_size),
         out_shape=jax.ShapeDtypeStruct((blocks_here, 4, 2 * block_points, bins_here), bf16),
-        in_specs=[VMEM] * 2 + [HBM] + [VMEM] * 2,
+        in_specs=[VMEM] * 4,
         out_specs=VMEM,
         scratch_shapes=[
-            pltpu.VMEM((blocks_here, block_points * strain_rows + 64, bins_here), bf16),
             pltpu.VMEM((points_here, 8 * strain_rows + 64), f32),
-            pltpu.SemaphoreType.DMA((blocks_here,)),
         ],
         compiler_params=params(),
         cost_estimate=cost(2 * points_here * strain_rows * bins_here, 6_000_000),
         name="green",
-    )(live, head, *in_hbm(strain_lines), scale_here, mechanism_here)
+    )(
+        live,
+        pltpu.with_memory_space_constraint(strain_lines, pltpu.VMEM),
+        scale_here,
+        mechanism_here,
+    )
 
     sent = spectra_call(1, onset_scale, slip_scale, live, green, received[1:], "spectra")
     gathered = exchange([None] + list(sent))

time: 22 us -> 22.3 us (1.014)
  waiting for transfers between devices: 2.97 us -> 4.18 us
  Pallas kernels: 8.52 us -> 7.74 us
    ppermute x6, waiting for transfers between devices: 1.73 us -> 2.94 us  [swap(): return lax.ppermute(value, 'pt', [(i, i ^ step) for i in range(pt_size)])]
    pallas_call x1, Pallas kernels: 2.85 us -> 2.2 us  [body(): pl.pallas_call(functools.partial(green_kernel, pt_size), out_shape=jax.Sh...]
  transfers between devices with their start and end apart: 7 -> 7, of which waited for: 4 -> 4; matrix products, arithmetic and copies ran while one was open for 0% -> 0% of each run, Pallas kernels for 19% -> 16%
where the time goes in v3:
time: 22.3 us
  starting transfers between devices  10.2 us (46%)
  Pallas kernels  7.74 us (35%)
  waiting for transfers between devices  4.18 us (19%)
    ppermute x6, starting transfers between devices, swap(): return lax.ppermute(value, 'pt', [(i, i ^ step) for i in range(pt_size)])  10.1 us
    ppermute x6, waiting for transfers between devices, swap(): return lax.ppermute(value, 'pt', [(i, i ^ step) for i in range(pt_size)])  2.94 us
    pallas_call x2, Pallas kernels, spectra_call(): pl.pallas_call(functools.partial(spectra_kernel, blocks_here, 4 * bins_he...  2.69 us
    pallas_call x1, Pallas kernels, body(): pl.pallas_call(functools.partial(green_kernel, pt_size), out_shape=jax.Sh...  2.2 us
    ppermute x1, waiting for transfers between devices, body(): other = lax.ppermute(excess, 'cmp', [(0, 1), (1, 0)])  1.24 us
    pallas_call x1, Pallas kernels, body(): pl.pallas_call(functools.partial(pack_kernel, blocks_here, block_points,...  1.2 us
    pallas_call x1, Pallas kernels, body(): pl.pallas_call(merge_kernel, out_shape=jax.ShapeDtypeStruct(high_band.sha...  0.83 us
    pallas_call x1, Pallas kernels, body(): pl.pallas_call(functools.partial(band_kernel, bins, samples), out_shape=[...  0.74 us
  transfers between devices with their start and end apart: 7, of which 4 were waited for; matrix products, arithmetic and copies ran while one was open for 0% of the time, Pallas kernels for 16%

profile of v3, /device:TPU:0, one launch (start us, length us, event | category | flops | bytes accessed | tf_op | source)
XLA Modules:
  0.0 22.3 jit_solution(6042116290223084095)
XLA Ops:
  0.0 1.2 %pack.1 = (s16[5,2,16,128]{3,2,1,0:T(8,128)(2,1)S(1)}, s16[5,2,16,128]{3,2,1,0:T(8,128)(2,1)S(1)}, s16[5,2,16,128]{3,2,1,0:T(8,128)(2,1)S(1)}, s16[5,2,16,128]{3...) custom-call(s32[4]{0:T(128)} %refs_0_.1, s32[4,12]{1,0:T(4,128)} %refs_1_.1, ...), custom_call_target="tpu_custom_call" | custom-call | tf_op jit(solution)/shard_map/pack/pallas_call | solution.py:433
  1.2 4.3 %collective-permute-start = (s16[5,2,16,128]{3,2,1,0:T(8,128)(2,1)S(1)}, s16[5,2,16,128]{3,2,1,0:T(8,128)(2,1)S(1)}, u32[]{:S(2)}, u32[]{:S(2)}) collective-permute-start(s16[5,2,16,128]{3,2,1,0:T(8,128)(2,1)S(1)} %get-tuple-element.21), channel_id=1, source_target_pairs={{0,8},{4,12},{8,0},{12,4},{1,9},{5,13},{9,1},{13,5},{2,10},{6,14},... | collective-permute-start | bytes 122888 | tf_op jit(solution)/shard_map/ppermute | solution.py:463
  5.5 1.1 %collective-permute-start.1 = (s16[5,2,16,128]{3,2,1,0:T(8,128)(2,1)S(1)}, s16[5,2,16,128]{3,2,1,0:T(8,128)(2,1)S(1)}, u32[]{:S(2)}, u32[]{:S(2)}) collective-permute-start(s16[5,2,16,128]{3,2,1,0:T(8,128)(2,1)S(1)} %get-tuple-element.22), channel_id=1, source_target_pairs={{0,12},{4,8},{8,4},{12,0},{1,13},{5,9},{9,5},{13,1},{2,14},{6,10},... | collective-permute-start | bytes 122888 | tf_op jit(solution)/shard_map/ppermute | solution.py:463
  6.6 0.2 %collective-permute-start.2 = (s16[5,2,16,128]{3,2,1,0:T(8,128)(2,1)S(1)}, s16[5,2,16,128]{3,2,1,0:T(8,128)(2,1)S(1)}, u32[]{:S(2)}, u32[]{:S(2)}) collective-permute-start(s16[5,2,16,128]{3,2,1,0:T(8,128)(2,1)S(1)} %get-tuple-element.23), channel_id=1, source_target_pairs={{0,4},{4,0},{8,12},{12,8},{1,5},{5,1},{9,13},{13,9},{2,6},{6,2},{1... | collective-permute-start | bytes 122888 | tf_op jit(solution)/shard_map/ppermute | solution.py:463
  6.9 2.2 %green.1.green_ref = bf16[5,4,256,128]{3,2,1,0:T(8,128)(2,1)S(1)} custom-call(s32[1,8,128]{2,1,0:T(8,128)S(1)} %get-tuple-element.18.live_ref, bf16[15360,128]{1,0:T(8,128)(2,1)S(1)} %bitcast.2, f32[5,24]{1,0:T(8,128)S(1)} %get-tuple-element.19.scale_ref, f32[6,640]{1,0:T(8,128)S(1)} %get-tuple-element.20.mechanism_ref), custom_call_target="tpu_custom_call" | custom-call | flops 3932160 | bytes 6000000 | tf_op jit(solution)/shard_map/green/pallas_call | solution.py:471
  9.1 0.0 copy-start.3
  9.1 0.0 copy-start.4
  9.1 0.0 copy-start.5
  9.1 0.0 copy-start.6
  9.1 0.0 copy-start.7
  9.1 2.2 %collective-permute-done.1.refs_1_ = s16[5,2,16,128]{3,2,1,0:T(8,128)(2,1)S(1)} collective-permute-done((s16[5,2,16,128]{3,2,1,0:T(8,128)(2,1)S(1)}, s16[5,2,16,128]{3,2,1,0:T(8,128)(2,1)S(1)}, u32[]{:S(2)}, u32[]{:S(2)}) %collective-permute-start.1) | collective-permute-done | bytes 40992 | tf_op jit(solution)/shard_map/ppermute | solution.py:463
  11.3 2.0 %spectra.1 = (f32[4,16,128]{2,1,0:T(8,128)S(1)}, f32[4,16,128]{2,1,0:T(8,128)S(1)}, f32[4,16,128]{2,1,0:T(8,128)S(1)}) custom-call(s32[1,8,128]{2,1,0:T(8,128)S(1)} %get-tuple-element.18.live_ref, bf16[5,4,256,128]{3,2,1,0:T(8,128)(2,1)S(1)} %green.1.green_ref, s16[5,2,16,128]{3,2,1,0:T(8,128)(2,1)S(1)} %collective-permute-done.refs_0_, ...), custom_call_target="tpu_custom_call" | custom-call | flops 3000000000 | bytes 12000000 | tf_op jit(solution)/shard_map/spectra/pallas_call | solution.py:329
  13.3 0.0 copy-start.1
  13.4 0.0 copy-start.2
  13.4 1.6 %collective-permute-start.3 = (f32[4,16,128]{2,1,0:T(8,128)S(1)}, f32[4,16,128]{2,1,0:T(8,128)S(1)}, u32[]{:S(2)}, u32[]{:S(2)}) collective-permute-start(f32[4,16,128]{2,1,0:T(8,128)S(1)} %get-tuple-element.24), channel_id=1, source_target_pairs={{0,12},{4,8},{8,4},{12,0},{1,13},{5,9},{9,5},{13,1},{2,14},{6,10},... | collective-permute-start | bytes 98312 | tf_op jit(solution)/shard_map/ppermute | solution.py:463
  15.0 2.8 %collective-permute-start.5 = (f32[4,16,128]{2,1,0:T(8,128)S(1)}, f32[4,16,128]{2,1,0:T(8,128)S(1)}, u32[]{:S(2)}, u32[]{:S(2)}) collective-permute-start(f32[4,16,128]{2,1,0:T(8,128)S(1)} %get-tuple-element.26), channel_id=1, source_target_pairs={{0,4},{4,0},{8,12},{12,8},{1,5},{5,1},{9,13},{13,9},{2,6},{6,2},{1... | collective-permute-start | bytes 98312 | tf_op jit(solution)/shard_map/ppermute | solution.py:463
  17.8 0.7 %own.1.refs_3_ = f32[4,16,128]{2,1,0:T(8,128)S(1)} custom-call(s32[1,8,128]{2,1,0:T(8,128)S(1)} %get-tuple-element.18.live_ref, bf16[5,4,256,128]{3,2,1,0:T(8,128)(2,1)S(1)} %green.1.green_ref, s16[5,2,16,128]{3,2,1,0:T(8,128)(2,1)S(1)} %get-tuple-element.27.refs_0_), custom_call_target="tpu_custom_call" | custom-call | flops 1000000000 | bytes 4000000 | tf_op jit(solution)/shard_map/own/pallas_call | solution.py:329
  18.5 0.7 %band.1 = (f32[32,512]{1,0:T(8,128)S(1)}, f32[8,512]{1,0:T(8,128)S(1)}) custom-call(s32[4]{0:T(128)S(1)} %copy-done.6, s32[4]{0:T(128)S(1)} %copy-done.7, f32[1,16,2,256]{3,2,1,0:T(2,128)S(1)} %copy-done.5, bf16[256,512]{1,0:T(8,128)(2,1)S(1)} %copy-done.3, bf16[256,512]{1,0:T(8,128)(2,1)S(1)} %copy-done.4), custom_call_target="tpu_custom_call" | custom-call | flops 25165824 | bytes 1000000 | tf_op jit(solution)/shard_map/band/pallas_call | solution.py:497
  19.3 0.7 %collective-permute-done.4.refs_1_ = f32[4,16,128]{2,1,0:T(8,128)S(1)} collective-permute-done((f32[4,16,128]{2,1,0:T(8,128)S(1)}, f32[4,16,128]{2,1,0:T(8,128)S(1)}, u32[]{:S(2)}, u32[]{:S(2)}) %collective-permute-start.4) | collective-permute-done | bytes 32800 | tf_op jit(solution)/shard_map/ppermute | solution.py:463
  20.0 0.1 collective-permute-done.5.refs_2_
  20.1 0.1 excess.1.own_ref
  20.2 0.1 collective-permute-start.6
  20.2 1.2 %collective-permute-done.6.other_ref = f32[32,512]{1,0:T(8,128)S(1)} collective-permute-done((f32[32,512]{1,0:T(8,128)S(1)}, f32[32,512]{1,0:T(8,128)S(1)}, u32[]{:S(2)}, u32[]{:S(2)}) %collective-permute-start.6) | collective-permute-done | bytes 65568 | tf_op jit(solution)/shard_map/ppermute | solution.py:518
  21.5 0.8 %merge.1 = f32[1,16,2,256]{3,2,1,0:T(2,128)} custom-call(f32[32,512]{1,0:T(8,128)S(1)} %excess.1.own_ref, f32[32,512]{1,0:T(8,128)S(1)} %collective-permute-done.6.other_ref, f32[8,512]{1,0:T(8,128)S(1)} %get-tuple-element.28.weight_ref, f32[1,16,2,256]{3,2,1,0:T(2,128)S(1)} %copy-done.5, bf16[512,256]{1,0:T(8,128)(2,1)S(1)} %copy-done.1, ...), custom_call_target="tpu_custom_call" | custom-call | tf_op jit(solution)/shard_map/merge/pallas_call | solution.py:520
  (13 shorter events, 0.0 us)
Async XLA Ops:
  0.0 6.9 %copy-start = (bf16[640,24,128]{2,1,0:T(8,128)(2,1)S(1)}, bf16[640,24,128]{2,1,0:T(8,128)(2,1)}, u32[]{:S(2)}) copy-start(bf16[640,24,128]{2,1,0:T(8,128)(2,1)} %param.14) | copy-start | bytes 11796484
  1.2 7.9 %collective-permute-start = (s16[5,2,16,128]{3,2,1,0:T(8,128)(2,1)S(1)}, s16[5,2,16,128]{3,2,1,0:T(8,128)(2,1)S(1)}, u32[]{:S(2)}, u32[]{:S(2)}) collective-permute-start(s16[5,2,16,128]{3,2,1,0:T(8,128)(2,1)S(1)} %get-tuple-element.21), channel_id=1, source_target_pairs={{0,8},{4,12},{8,0},{12,4},{1,9},{5,13},{9,1},{13,5},{2,10},{6,14},... | collective-permute-start | bytes 122888 | tf_op jit(solution)/shard_map/ppermute | solution.py:463
  5.5 5.8 %collective-permute-start.1 = (s16[5,2,16,128]{3,2,1,0:T(8,128)(2,1)S(1)}, s16[5,2,16,128]{3,2,1,0:T(8,128)(2,1)S(1)}, u32[]{:S(2)}, u32[]{:S(2)}) collective-permute-start(s16[5,2,16,128]{3,2,1,0:T(8,128)(2,1)S(1)} %get-tuple-element.22), channel_id=1, source_target_pairs={{0,12},{4,8},{8,4},{12,0},{1,13},{5,9},{9,5},{13,1},{2,14},{6,10},... | collective-permute-start | bytes 122888 | tf_op jit(solution)/shard_map/ppermute | solution.py:463
  6.6 4.7 %collective-permute-start.2 = (s16[5,2,16,128]{3,2,1,0:T(8,128)(2,1)S(1)}, s16[5,2,16,128]{3,2,1,0:T(8,128)(2,1)S(1)}, u32[]{:S(2)}, u32[]{:S(2)}) collective-permute-start(s16[5,2,16,128]{3,2,1,0:T(8,128)(2,1)S(1)} %get-tuple-element.23), channel_id=1, source_target_pairs={{0,4},{4,0},{8,12},{12,8},{1,5},{5,1},{9,13},{13,9},{2,6},{6,2},{1... | collective-permute-start | bytes 122888 | tf_op jit(solution)/shard_map/ppermute | solution.py:463
  9.1 9.4 %copy-start.3 = (bf16[256,512]{1,0:T(8,128)(2,1)S(1)}, bf16[256,512]{1,0:T(8,128)(2,1)}, u32[]{:S(2)}) copy-start(bf16[256,512]{1,0:T(8,128)(2,1)} %constant.8.clone.table_high) | copy-start | bytes 786436
  9.1 9.4 %copy-start.4 = (bf16[256,512]{1,0:T(8,128)(2,1)S(1)}, bf16[256,512]{1,0:T(8,128)(2,1)}, u32[]{:S(2)}) copy-start(bf16[256,512]{1,0:T(8,128)(2,1)} %constant.9.clone.table_low) | copy-start | bytes 786436
  9.1 9.4 %copy-start.5 = (f32[1,16,2,256]{3,2,1,0:T(2,128)S(1)}, f32[1,16,2,256]{3,2,1,0:T(2,128)}, u32[]{:S(2)}) copy-start(f32[1,16,2,256]{3,2,1,0:T(2,128)} %high_ref.3) | copy-start | bytes 98308
  9.1 9.4 %copy-start.6 = (s32[4]{0:T(128)S(1)}, s32[4]{0:T(128)}, u32[]{:S(2)}) copy-start(s32[4]{0:T(128)} %refs_0_.1) | copy-start | bytes 52
  9.1 9.4 %copy-start.7 = (s32[4]{0:T(128)S(1)}, s32[4]{0:T(128)}, u32[]{:S(2)}) copy-start(s32[4]{0:T(128)} %crossover_ref.1) | copy-start | bytes 52
  13.3 8.1 %copy-start.1 = (bf16[512,256]{1,0:T(8,128)(2,1)S(1)}, bf16[512,256]{1,0:T(8,128)(2,1)}, u32[]{:S(2)}) copy-start(bf16[512,256]{1,0:T(8,128)(2,1)} %constant.10.clone.table_high) | copy-start | bytes 786436
  13.4 8.1 %copy-start.2 = (bf16[512,256]{1,0:T(8,128)(2,1)S(1)}, bf16[512,256]{1,0:T(8,128)(2,1)}, u32[]{:S(2)}) copy-start(bf16[512,256]{1,0:T(8,128)(2,1)} %constant.11.clone.table_low) | copy-start | bytes 786436
  13.4 5.9 %collective-permute-start.3 = (f32[4,16,128]{2,1,0:T(8,128)S(1)}, f32[4,16,128]{2,1,0:T(8,128)S(1)}, u32[]{:S(2)}, u32[]{:S(2)}) collective-permute-start(f32[4,16,128]{2,1,0:T(8,128)S(1)} %get-tuple-element.24), channel_id=1, source_target_pairs={{0,12},{4,8},{8,4},{12,0},{1,13},{5,9},{9,5},{13,1},{2,14},{6,10},... | collective-permute-start | bytes 98312 | tf_op jit(solution)/shard_map/ppermute | solution.py:463
  15.0 5.0 %collective-permute-start.4 = (f32[4,16,128]{2,1,0:T(8,128)S(1)}, f32[4,16,128]{2,1,0:T(8,128)S(1)}, u32[]{:S(2)}, u32[]{:S(2)}) collective-permute-start(f32[4,16,128]{2,1,0:T(8,128)S(1)} %get-tuple-element.25), channel_id=1, source_target_pairs={{0,8},{4,12},{8,0},{12,4},{1,9},{5,13},{9,1},{13,5},{2,10},{6,14},... | collective-permute-start | bytes 98312 | tf_op jit(solution)/shard_map/ppermute | solution.py:463
  15.0 5.1 %collective-permute-start.5 = (f32[4,16,128]{2,1,0:T(8,128)S(1)}, f32[4,16,128]{2,1,0:T(8,128)S(1)}, u32[]{:S(2)}, u32[]{:S(2)}) collective-permute-start(f32[4,16,128]{2,1,0:T(8,128)S(1)} %get-tuple-element.26), channel_id=1, source_target_pairs={{0,4},{4,0},{8,12},{12,8},{1,5},{5,1},{9,13},{13,9},{2,6},{6,2},{1... | collective-permute-start | bytes 98312 | tf_op jit(solution)/shard_map/ppermute | solution.py:463
  20.2 1.3 %collective-permute-start.6 = (f32[32,512]{1,0:T(8,128)S(1)}, f32[32,512]{1,0:T(8,128)S(1)}, u32[]{:S(2)}, u32[]{:S(2)}) collective-permute-start(f32[32,512]{1,0:T(8,128)S(1)} %excess.1.own_ref), channel_id=1, source_target_pairs={{0,1},{1,0},{2,3},{3,2},{4,5},{5,4},{6,7},{7,6},{8,9},{9,8},{10,11... | collective-permute-start | bytes 196616 | tf_op jit(solution)/shard_map/ppermute | solution.py:518
